TPU v7x, 32 devices: a whole 2x2x4 slice. The times are simulated.
32 devices in a mesh: gx: 4 (over y, x), gy: 8 (over z, core).
Axes of the slice: x: 2, y: 2, z: 4, core: 2. Of those that a mesh axis runs over, the one named last changes fastest.
Arguments:
- old_fields: float32 [4, 128, 128, 128], P(None, 'gx', 'gy'), may hold values from -12 to 12, as said below
- inverse_step: float32 [128, 128, 128], P('gx', 'gy'), may hold values from 8 to 64
- boundary: int32 [128, 128, 128], P('gx', 'gy'), may hold values from 0 to 1, as said below
Outputs:
- new_fields: float32 [4, 128, 128, 128], P(None, 'gx', 'gy')
- pressure: float32 [128, 128, 128], P('gx', 'gy')
Inputs may be any that keep to these rules, and one draw needn't show every extreme that they name: `old_fields`: drawn with a random sign and a magnitude that may vary over the brick. `boundary`: all copies of one mesh node hold the same value; the lowest node layer of every column and the top node plane are 0, and a column may have up to three fixed bottom layers.
All inputs are finite; a program needn't handle non-finite values.
Results may differ from a plain program's by a relative error of at most 0.00012.
Values sent between devices are 32-bit elements; how exact they have to be, the bound alone decides.
No kernel may reach another device: no remote copies, remote signals or barrier semaphores. Data moves between devices by JAX's collectives and lax.ppermute only.
A program may use at most 64 MiB of HBM per device.

v0:
```python
import functools

import jax
import jax.numpy as jnp
import numpy as np
from jax import lax
from jax.experimental import pallas as pl
from jax.experimental.pallas import tpu as pltpu
from jax.sharding import PartitionSpec as P

ITERS = 6
CHEB = 6

SIGMA_SHIFT = 0.5
DIFFUSE = (1.0, 1.0, 1.0, 1.4)
COUPLING = 1.0
STRATIFY = 1.0
SPREAD = 20.0
STEP_MAX = 64.0
INTERVAL_SHARE = 0.82
HIGHEST_PRECISION = lax.Precision.HIGHEST
LOBATTO_POINTS = (
    -1.0,
    -0.8717401485096066,
    -0.5917001814331423,
    -0.2092992179024789,
    0.2092992179024789,
    0.5917001814331423,
    0.8717401485096066,
    1.0,
)


def legendre_value(points, degree):
    previous = points * 0.0 + 1.0
    current = points
    for order in range(1, degree):
        following = ((2 * order + 1) * points * current - order * previous) / (order + 1)
        previous = current
        current = following
    return current


def quadrature_tables():
    degree = 7
    points = np.array(LOBATTO_POINTS)
    values = legendre_value(points, degree)
    weights = 2.0 / (degree * (degree + 1) * values * values)
    derive = np.zeros((degree + 1, degree + 1))
    for row_index in range(degree + 1):
        for column_index in range(degree + 1):
            if row_index != column_index:
                derive[row_index, column_index] = values[row_index] / (
                    values[column_index] * (points[row_index] - points[column_index])
                )
    derive[0, 0] = -degree * (degree + 1) / 4.0
    derive[degree, degree] = degree * (degree + 1) / 4.0
    stiffness_table = derive.T @ (weights[:, None] * derive)
    return (weights, derive, stiffness_table)


WEIGHTS, DERIVE, STIFF = quadrature_tables()
SLOPE = WEIGHTS[:, None] * DERIVE
COPIES = np.where(np.arange(8) % 7 == 0, 2.0, 1.0)


def chebyshev_bounds():
    weight_matrix = np.eye(8) * WEIGHTS

    def kron3(a, b, c):
        return np.kron(np.kron(a, b), c)

    element_matrix = (
        kron3(STIFF, weight_matrix, weight_matrix)
        + kron3(weight_matrix, STIFF, weight_matrix)
        + kron3(weight_matrix, weight_matrix, STIFF)
        + SIGMA_SHIFT * kron3(weight_matrix, weight_matrix, weight_matrix)
    )
    bounds_ratio = np.sum(np.abs(element_matrix), axis=1) / np.diagonal(element_matrix)
    upper_bound = float(np.max(bounds_ratio))
    lower_bound = upper_bound / SPREAD
    return ((upper_bound + lower_bound) / 2.0, (upper_bound - lower_bound) / 2.0)


def spectrum_top(diffuse):
    root = np.sqrt(COPIES)
    stiff = root[:, None] * STIFF * root[None, :]
    weight = np.diag(WEIGHTS * COPIES)

    def kron3(a, b, c):
        return np.kron(np.kron(a, b), c)

    element = diffuse * (
        kron3(stiff, weight, weight) + kron3(weight, stiff, weight) + kron3(weight, weight, stiff)
    ) + STEP_MAX * kron3(weight, weight, weight)
    return float(np.linalg.eigvalsh(element)[-1])


def line_sums(table, length):
    matrix = np.kron(np.eye(length // 8), table)
    total = matrix.copy()
    for start in range(8, length, 8):
        total[start] += matrix[start - 1]
        total[start - 1] += matrix[start]
    return total


def depth_line(vector, length):
    line = np.tile(vector * COPIES, length // 8)
    line[0] = vector[0]
    line[-1] = vector[-1]
    return line


def f32(array):
    return np.ascontiguousarray(array, np.float32)


def rolled_rows(table):
    out = np.zeros((8, 8, 128))
    for shift in range(8):
        for row in range(8):
            out[shift, row] = table[row, (row - shift) % 8]
    return out


def block(a, b, c):
    return a[:, None, None] * b[:, None] * c


class Tables:
    def __init__(self, depth):
        ones8, ones = np.ones(8), np.ones(depth)
        wide = WEIGHTS * COPIES
        deep = depth_line(WEIGHTS, depth)
        flat = np.tile(WEIGHTS, depth // 8)
        stiff = np.diagonal(STIFF)
        wide_s, deep_s = stiff * COPIES, depth_line(stiff, depth)
        share = 1.0 / COPIES
        share_z = np.tile(share, depth // 8)
        share_z[0] = share_z[-1] = 1.0
        self.summed = f32(
            np.stack([block(ones8, wide, deep), block(wide, ones8, deep), block(wide, wide, ones)])
        )
        self.local = f32(
            np.stack(
                [block(ones8, WEIGHTS, flat), block(WEIGHTS, ones8, flat), block(WEIGHTS, WEIGHTS, ones)]
            )
        )
        self.share = f32(block(share, share, share_z))
        diagonal = (
            block(wide_s, wide, deep)
            + block(wide, wide_s, deep)
            + block(wide, wide, deep_s)
            + SIGMA_SHIFT * block(wide, wide, deep)
        )
        self.inverse = f32(1.0 / diagonal)
        self.shift = f32(SIGMA_SHIFT * block(wide, wide, deep))
        self.stiff_y = f32(rolled_rows(STIFF))
        self.slope_y = f32(rolled_rows(SLOPE))
        self.stiff_z = f32(line_sums(STIFF, depth).T)
        self.plain_z = f32(np.kron(np.eye(depth // 8), STIFF).T)
        self.slope_z = f32(line_sums(SLOPE, depth).T)


def row_marks():
    row = lax.broadcasted_iota(jnp.int32, (8, 128), 0)
    return jnp.where(row == 0, 1.0, 0.0), jnp.where(row == 7, 1.0, 0.0)


def by_place(vector, place):
    out = jnp.full(place.shape, float(vector[0]), jnp.float32)
    for i in range(1, 8):
        out = jnp.where(place == i, float(vector[i]), out)
    return out


def along_x(rows, table):
    if np.allclose(table, table[::-1, ::-1]):
        even = 0.5 * (table[:4, :4] + table[:4, :3:-1])
        odd = 0.5 * (table[:4, :4] - table[:4, :3:-1])
        plus = [rows[i] + rows[7 - i] for i in range(4)]
        minus = [rows[i] - rows[7 - i] for i in range(4)]
        out = [None] * 8
        for a in range(4):
            p = sum(float(even[a, b]) * plus[b] for b in range(4))
            m = sum(float(odd[a, b]) * minus[b] for b in range(4))
            out[a], out[7 - a] = p + m, p - m
        return out
    return [sum(float(table[a, b]) * rows[b] for b in range(8)) for a in range(8)]


def along_y(tiles, factors):
    total = factors[0] * tiles
    for shift in range(1, 8):
        total = total + factors[shift] * pltpu.roll(tiles, shift, axis=1)
    return total


def along_z(tiles, matrix):
    x, y, z = tiles.shape
    out = jnp.dot(
        tiles.reshape(x * y, z), matrix, precision=HIGHEST_PRECISION, preferred_element_type=jnp.float32
    )
    return out.reshape(x, y, z)


def join_y(parts, low, high):
    out = list(parts)
    for e in range(1, len(parts)):
        out[e - 1] = out[e - 1] + high * pltpu.roll(parts[e], 7, axis=1)
        out[e] = out[e] + low * pltpu.roll(parts[e - 1], 1, axis=1)
    return out


def spread_rows(rows):
    return jnp.broadcast_to(rows[:, None, :], (rows.shape[0], 8, rows.shape[1]))


def column_sums(x_rows, y_parts, z_parts, summed, edges):
    y_parts = join_y(y_parts, edges[0], edges[1])
    return [
        jnp.stack(kx) * summed[0, 0] + ky * summed[1] + kz * summed[2]
        for kx, ky, kz in zip(x_rows, y_parts, z_parts)
    ]


def emit_column(ex, x_rows, y_parts, z_parts, summed, edges, out, state, finish=None, factor=None):
    rows = pl.ds(8 * ex, 8)
    parts = column_sums(x_rows, y_parts, z_parts, summed, edges)
    for e, part in enumerate(parts):
        ys = pl.ds(8 * e, 8)
        out[rows, ys] = part if finish is None else finish(e, part)
        if ex:
            for row, face in ((8 * ex, state[e]), (8 * ex - 1, x_rows[e][0])):
                face = face * summed[0, 0]
                out[row, ys] += face if factor is None else face * factor(row, ys)
    return [r[7] for r in x_rows]


def end_rows(table):
    row = lax.broadcasted_iota(jnp.int32, (8, 128), 0)
    return (table[0], table[7]), (by_place(table[0], row), by_place(table[7], row))


def store_faces(ex, e, columns, count, tile, even, ends, faces, x=True, y=True):
    x_near, x_far, y_near, y_far = faces
    (x_low, x_high), (y_low, y_high) = ends
    rows, ys = pl.ds(8 * ex, 8), pl.ds(8 * e, 8)
    if x and ex == 0:
        low = sum(float(x_low[i]) * tile[i] for i in range(8))
        x_near[ys] = low
        x_far[ys] = low
    if x and ex == columns - 1:
        high = sum(float(x_high[i]) * tile[i] for i in range(8))
        x_near[ys] = jnp.where(even[0], high, x_near[ys])
        x_far[ys] = jnp.where(even[0], x_far[ys], high)
    if y and e == 0:
        low = jnp.sum(tile * y_low, axis=1)
        y_near[rows] = low
        y_far[rows] = low
    if y and e == count - 1:
        high = jnp.sum(tile * y_high, axis=1)
        y_near[rows] = jnp.where(even[1], high, y_near[rows])
        y_far[rows] = jnp.where(even[1], y_far[rows], high)


def parity(even_ref):
    return even_ref[0] > 0.5, even_ref[1] > 0.5


def before_of(even, near, far):
    return jnp.where(even, far, near)


def after_of(even, near, far):
    return jnp.where(even, near, far)


def with_faces(tile, ex, e, columns, count, received, even, edges, weight_x=None, weight_y=None, mask=None):
    x_far, x_near, y_far, y_near = received
    rows, ys = pl.ds(8 * ex, 8), pl.ds(8 * e, 8)

    def weighted(face, weight):
        return face if weight is None else face * weight

    if e == 0:
        face = before_of(even[1], y_near[rows], y_far[rows])
        face = spread_rows(face) * weighted(edges[0], weight_y)
        tile = tile + weighted(face, mask)
    if e == count - 1:
        face = after_of(even[1], y_near[rows], y_far[rows])
        face = spread_rows(face) * weighted(edges[1], weight_y)
        tile = tile + weighted(face, mask)
    if ex == 0:
        face = before_of(even[0], x_near[ys], x_far[ys])
        face = weighted(face, weight_x) if mask is None else weighted(face, weight_x) * mask[0]
        tile = jnp.concatenate([tile[0:1] + face[None], tile[1:]], axis=0)
    if ex == columns - 1:
        face = after_of(even[0], x_near[ys], x_far[ys])
        face = weighted(face, weight_x) if mask is None else weighted(face, weight_x) * mask[7]
        tile = jnp.concatenate([tile[:7], tile[7:8] + face[None]], axis=0)
    return tile


def split_rows(block_rows):
    return [block_rows[i] for i in range(8)]


def load_local(old_far, step_far, even_ref, out, x_near, x_far, y_near, y_far, old, step, arrived):
    columns, count, depth = out.shape[1] // 8, out.shape[2] // 8, out.shape[3]
    copies = [pltpu.make_async_copy(step_far, step, arrived.at[4])]
    copies += [pltpu.make_async_copy(old_far.at[i], old.at[i], arrived.at[i]) for i in range(4)]
    for copy in copies:
        copy.start()
    even, edges = parity(even_ref), row_marks()
    row = lax.broadcasted_iota(jnp.int32, (8, depth), 0)
    lane = lax.broadcasted_iota(jnp.int32, (8, depth), 1)
    place = lane & 7
    after = jnp.where((place == 0) & (lane > 0), 1.0, 0.0)
    before_z = jnp.where((place == 7) & (lane < depth - 1), 1.0, 0.0)
    plane = by_place(WEIGHTS, row) * by_place(WEIGHTS, place)
    mass = jnp.stack([float(w) * plane for w in WEIGHTS])
    for field in (4, 0, 1, 2, 3):
        if field != 3:
            copies[0 if field == 4 else field + 1].wait()
        if field == 2:
            copies[4].wait()
        before = [None] * count
        for ex in range(columns):
            rows = pl.ds(8 * ex, 8)
            parts = []
            for e in range(count):
                ys = pl.ds(8 * e, 8)
                value = step[rows, ys]
                if field < 4:
                    value = value * old[field, rows, ys]
                if field == 2:
                    value = value + COUPLING * old[3, rows, ys]
                if field == 3:
                    value = value - STRATIFY * old[2, rows, ys]
                value = value * mass
                value = (
                    value
                    + after * pltpu.roll(value, 1, axis=2)
                    + before_z * pltpu.roll(value, depth - 1, axis=2)
                )
                parts.append(value)
            parts = join_y(parts, edges[0], edges[1])
            for e in range(count):
                ys = pl.ds(8 * e, 8)
                out[field, rows, ys] = parts[e]
                if ex:
                    out[field, 8 * ex, ys] += before[e]
                    out[field, 8 * ex - 1, ys] += parts[e][0]
                before[e] = parts[e][7]
        for e in range(count):
            ys = pl.ds(8 * e, 8)
            low, high = out[field, 0, ys], out[field, 8 * columns - 1, ys]
            x_near[field, ys] = jnp.where(even[0], high, low)
            x_far[field, ys] = jnp.where(even[0], low, high)
        for ex in range(columns):
            rows = pl.ds(8 * ex, 8)
            low = out[field, rows, pl.ds(0, 8)][:, 0]
            high = out[field, rows, pl.ds(8 * count - 8, 8)][:, 7]
            y_near[field, rows] = jnp.where(even[1], high, low)
            y_far[field, rows] = jnp.where(even[1], low, high)


def fix_corners(y_near, y_far, x_near, x_far, even_ref, near, far):
    length = y_near.shape[1]
    last = x_near.shape[1] - 1
    even = [even_ref[0, 0:1] > 0.5, even_ref[1, 0:1] > 0.5]
    near[...] = y_near[...]
    far[...] = y_far[...]
    for field in range(5):
        for end, place in ((before_of, 0), (after_of, length - 1)):
            first = end(even[0], x_near[field, 0:1], x_far[field, 0:1])
            final = end(even[0], x_near[field, last : last + 1], x_far[field, last : last + 1])
            near[field, place : place + 1] += jnp.where(even[1], final, first)
            far[field, place : place + 1] += jnp.where(even[1], first, final)


def stiff_terms(tiles, stiff_y, stiff_z):
    x_rows = [along_x(split_rows(t), STIFF) for t in tiles]
    y_parts = [along_y(t, stiff_y) for t in tiles]
    z_all = along_z(jnp.concatenate(tiles, axis=0), stiff_z[...])
    z_parts = [z_all[8 * e : 8 * e + 8] for e in range(len(tiles))]
    return x_rows, y_parts, z_parts


def field_faces(c, ex, e, columns, count, tile, even, ends, slope_ends, faces):
    store_faces(ex, e, columns, count, tile, even, ends, [f.at[c] for f in faces])
    slopes = [f.at[4] for f in faces]
    if isinstance(c, int):
        store_faces(ex, e, columns, count, tile, even, slope_ends, slopes, c == 0, c == 1)
        return

    @pl.when(c == 0)
    def _():
        store_faces(ex, e, columns, count, tile, even, slope_ends, slopes, True, False)

    @pl.when(c == 1)
    def _():
        store_faces(ex, e, columns, count, tile, even, slope_ends, slopes, False, True)


def start_field(local, boundary, x_far, x_near, y_far, y_near, even_ref, right, *faces):
    columns, count = right.shape[1] // 8, right.shape[2] // 8
    even, edges = parity(even_ref), row_marks()
    received = (x_far, x_near, y_far, y_near)
    ends, slope_ends = end_rows(STIFF), end_rows(SLOPE)
    for c in range(4):
        for ex in range(columns):
            for e in range(count):
                rows, ys = pl.ds(8 * ex, 8), pl.ds(8 * e, 8)
                tile = with_faces(local[c, rows, ys], ex, e, columns, count, [r.at[c] for r in received],
                                  even, edges)
                tile = tile * boundary[rows, ys].astype(jnp.float32)
                right[c, rows, ys] = tile
                field_faces(c, ex, e, columns, count, tile, even, ends, slope_ends, faces)


def pick(c, values):
    out = jnp.float32(values[0])
    for i in range(1, 4):
        out = jnp.where(c == i, jnp.float32(values[i]), out)
    return out


def start_sums(scales, rates, local, boundary, x_far, x_near, y_far, y_near, even_ref, right, summed, share, stiff_y,
               stiff_z, reaction, free, ahead, dots):
    columns, count = ahead.shape[1] // 8, ahead.shape[2] // 8
    even, edges = parity(even_ref), row_marks()
    received = [r.at[4] for r in (x_far, x_near, y_far, y_near)]
    for ex in range(columns):
        for e in range(count):
            rows, ys = pl.ds(8 * ex, 8), pl.ds(8 * e, 8)
            reaction[rows, ys] = with_faces(local[4, rows, ys], ex, e, columns, count, received, even, edges)
            free[rows, ys] = boundary[rows, ys].astype(jnp.float32)
    dots[...] = jnp.zeros_like(dots)
    basis_sums(scales, rates, right, None, reaction, free, summed, share, stiff_y, stiff_z, ahead, dots)


def basis_sums(scales, rates, newest, older, reaction, free, summed, share, stiff_y, stiff_z, ahead, dots):
    columns, count = ahead.shape[1] // 8, ahead.shape[2] // 8
    edges = row_marks()
    double = 1.0 if older is None else 2.0

    def component(c, carry):
        scale, rate = pick(c, [double * v for v in scales]), pick(c, [double * v for v in rates])
        same = jnp.zeros((8, 128), jnp.float32)
        cross = jnp.zeros((8, 128), jnp.float32)
        state = None
        for ex in range(columns):
            rows = pl.ds(8 * ex, 8)
            tiles = []
            for e in range(count):
                ys = pl.ds(8 * e, 8)
                tile = newest[c, rows, ys]
                weighted = tile * share[...]
                same = same + jnp.sum(weighted * tile, axis=0)
                if older is not None:
                    cross = cross + jnp.sum(weighted * older[c, rows, ys], axis=0)
                tiles.append(tile)
            x_rows, y_parts, z_parts = stiff_terms(tiles, stiff_y, stiff_z)

            def finish(e, part):
                ys = pl.ds(8 * e, 8)
                value = scale * part + (rate * reaction[rows, ys] - double) * tiles[e]
                value = value * free[rows, ys]
                return value if older is None else value - older[c, rows, ys]

            state = emit_column(ex, x_rows, y_parts, z_parts, summed, edges, ahead.at[c], state, finish,
                                lambda row, ys: scale * free[row, ys])
        dots[pl.ds(c, 1)] = jnp.sum(same, axis=0, keepdims=True)
        if older is not None:
            dots[pl.ds(c + 4, 1)] = jnp.sum(cross, axis=0, keepdims=True)
        return carry

    lax.fori_loop(0, 4, component, 0)


def next_field(c, ex, e, ahead, free, received, scale, summed, edges, even, columns, count):
    rows, ys = pl.ds(8 * ex, 8), pl.ds(8 * e, 8)
    return with_faces(ahead[c, rows, ys], ex, e, columns, count, [r.at[c] for r in received], even, edges,
                      summed[0, 0], summed[1], scale * free[rows, ys])


def grow_field(scales, ahead, free, x_far, x_near, y_far, y_near, even_ref, summed, out, *faces):
    received = (x_far, x_near, y_far, y_near)
    columns, count = out.shape[1] // 8, out.shape[2] // 8
    even, edges = parity(even_ref), row_marks()
    ends, slope_ends = end_rows(STIFF), end_rows(SLOPE)
    for c in range(4):
        for ex in range(columns):
            for e in range(count):
                tile = next_field(c, ex, e, ahead, free, received, scales[c], summed, edges, even, columns, count)
                out[c, pl.ds(8 * ex, 8), pl.ds(8 * e, 8)] = tile
                field_faces(c, ex, e, columns, count, tile, even, ends, slope_ends, faces)


def last_field(scales, rates, *refs):
    refs = list(refs)
    ahead, newest, reaction, free, *received, even_ref, summed, share, stiff_y, stiff_z, local = refs[:14]
    dots, (out, sums, *slopes) = refs[14:19], refs[19:]
    columns, count = out.shape[1] // 8, out.shape[2] // 8
    even, edges = parity(even_ref), row_marks()
    slope_ends = end_rows(SLOPE)
    for i in range(1, ITERS - 1):
        sums[i] = dots[i][...]
    for c in range(4):
        scale, rate = scales[c], rates[c]
        same = jnp.zeros((8, 128), jnp.float32)
        cross = jnp.zeros((8, 128), jnp.float32)
        work = jnp.zeros((8, 128), jnp.float32)
        for ex in range(columns):
            rows = pl.ds(8 * ex, 8)
            tiles = []
            for e in range(count):
                ys = pl.ds(8 * e, 8)
                tile = next_field(c, ex, e, ahead, free, received, 2.0 * scale, summed, edges, even, columns, count)
                now = newest[c, rows, ys]
                out[c, rows, ys] = tile
                store_faces(ex, e, columns, count, tile, even, slope_ends, slopes, c == 0, c == 1)
                weighted = tile * share[...]
                same = same + jnp.sum(weighted * tile, axis=0)
                cross = cross + jnp.sum(weighted * now, axis=0)
                extra = (rate * reaction[rows, ys] - 1.0) * tile
                work = work + jnp.sum(weighted * extra, axis=0)
                tiles.append(tile)
            x_rows, y_parts, z_parts = stiff_terms(tiles, stiff_y, stiff_z)
            for e in range(count):
                term = jnp.stack(x_rows[e]) * local[0] + y_parts[e] * local[1] + z_parts[e] * local[2]
                work = work + scale * jnp.sum(term * tiles[e], axis=0)
        sums[ITERS - 1, c : c + 1] = jnp.sum(same, axis=0, keepdims=True)
        sums[ITERS - 1, c + 4 : c + 5] = jnp.sum(cross, axis=0, keepdims=True)
        sums[0, c : c + 1] = dots[0][c : c + 1]
        sums[0, c + 4 : c + 5] = jnp.sum(work, axis=0, keepdims=True)


def finish_fields(halves, gain, *refs):
    sums, *basis = refs[: ITERS + 1]
    refs = refs[ITERS + 1 :]
    slopes = [[r.at[4] for r in refs[4 * k : 4 * k + 4]] for k in range(ITERS - 1)]
    refs = refs[4 * ITERS - 4 :]
    slopes.append(refs[:4])
    even_ref, free, summed, slope_y, slope_z, inverse = refs[4:10]
    fields, remainder, update, *faces = refs[10:17]
    weights, raw, *joined = refs[17:]
    columns, count = raw.shape[0] // 8, raw.shape[1] // 8
    even, edges = parity(even_ref), row_marks()
    ends = end_rows(STIFF)
    total = [jnp.broadcast_to(jnp.sum(sums[i], axis=1, keepdims=True), (8, 128)) for i in range(ITERS)]
    other = [pltpu.roll(t, 4, axis=0) for t in total]
    row = lax.broadcasted_iota(jnp.int32, (8, 128), 0)
    half = jnp.full((8, 128), halves[0], jnp.float32)
    for i in range(1, 4):
        half = jnp.where(row == i, halves[i], half)
    moments = [total[0], other[1]]
    for level in range(2, 2 * ITERS - 1):
        inner = total[level // 2] if level % 2 == 0 else other[level // 2 + 1]
        moments.append(2.0 * inner - moments[level % 2])
    top = 2.0 * other[0] - other[5]
    moments.append(2.0 * top - moments[1])
    for i, value in enumerate(conjugate_coefficients(moments, half, half)):
        weights[i] = value

    def combine(c, carry):
        factor = [weights[i, pl.ds(c, 1)] for i in range(ITERS)]
        for x in range(0, 8 * columns, 8):
            rows = pl.ds(x, 8)
            value = basis[0][c, rows] * factor[0][None]
            for i in range(1, ITERS):
                value = value + basis[i][c, rows] * factor[i][None]
            fields[c, rows] = value
        return carry

    lax.fori_loop(0, 4, combine, 0)
    for n in range(4):
        c = n // 2
        joined[n][...] = sum(slopes[i][n][...] * weights[i, c : c + 1] for i in range(ITERS))
    state = None
    for ex in range(columns):
        rows = pl.ds(8 * ex, 8)
        x_rows, y_parts, z_tiles = [], [], []
        for e in range(count):
            ys = pl.ds(8 * e, 8)
            x_rows.append(along_x(split_rows(fields[0, rows, ys]), SLOPE))
            y_parts.append(along_y(fields[1, rows, ys], slope_y))
            z_tiles.append(fields[2, rows, ys])
        z_all = along_z(jnp.concatenate(z_tiles, axis=0), slope_z[...])
        z_parts = [z_all[8 * e : 8 * e + 8] for e in range(count)]
        state = emit_column(ex, x_rows, y_parts, z_parts, summed, edges, raw, state)
    for ex in range(columns):
        for e in range(count):
            rows, ys = pl.ds(8 * ex, 8), pl.ds(8 * e, 8)
            tile = with_faces(raw[rows, ys], ex, e, columns, count, joined, even, edges, summed[0, 0], summed[1])
            left = -tile * free[rows, ys]
            change = gain * inverse[...] * left
            remainder[rows, ys] = left
            update[rows, ys] = change
            store_faces(ex, e, columns, count, change, even, ends, faces)


def pressure_sums(update, summed, shift, stiff_y, stiff_z, raw):
    columns, count = raw.shape[0] // 8, raw.shape[1] // 8
    edges = row_marks()
    state = None
    for ex in range(columns):
        rows = pl.ds(8 * ex, 8)
        tiles = [update[rows, pl.ds(8 * e, 8)] for e in range(count)]
        x_rows, y_parts, z_parts = stiff_terms(tiles, stiff_y, stiff_z)
        state = emit_column(ex, x_rows, y_parts, z_parts, summed, edges, raw, state,
                            lambda e, part: part + shift[...] * tiles[e])


def pressure_step(last, keep, gain, *refs):
    raw, free, *received, even_ref, summed, inverse, remainder_in, update_in, pressure_in = refs[:12]
    if last:
        pressure_far, pressure, left_here = refs[12:]
    else:
        pressure, remainder, update, *faces = refs[12:]
    columns, count = raw.shape[0] // 8, raw.shape[1] // 8
    copies = []
    even, edges = parity(even_ref), row_marks()
    ends = end_rows(STIFF)
    for ex in range(columns):
        for e in range(count):
            rows, ys = pl.ds(8 * ex, 8), pl.ds(8 * e, 8)
            tile = with_faces(raw[rows, ys], ex, e, columns, count, received, even, edges,
                              summed[0, 0], summed[1])
            left = remainder_in[rows, ys] - tile * free[rows, ys]
            change = gain * inverse[...] * left + keep * update_in[rows, ys]
            pressure[rows, ys] = pressure_in[rows, ys] + change
            if not last:
                remainder[rows, ys] = left
                update[rows, ys] = change
                store_faces(ex, e, columns, count, change, even, ends, faces)
        if last:
            rows = pl.ds(8 * ex, 8)
            copies.append(pltpu.make_async_copy(pressure.at[rows], pressure_far.at[rows], left_here.at[ex]))
            copies[-1].start()
    for copy in copies:
        copy.wait()


VMEM_BYTES = 24 * 1024 * 1024


def call(kernel, name, outs, *args, scratch=(), cost=None, far_in=0, far_out=0, copies=0):
    held, far = pl.BlockSpec(memory_space=pltpu.VMEM), pl.BlockSpec(memory_space=pltpu.HBM)
    scratch_shapes = [pltpu.VMEM(s, jnp.float32) for s in scratch]
    if copies:
        scratch_shapes.append(pltpu.SemaphoreType.DMA((copies,)))
    return pl.pallas_call(
        kernel,
        name=name,
        out_shape=[jax.ShapeDtypeStruct(s, jnp.float32) for s in outs],
        in_specs=[far] * far_in + [held] * (len(args) - far_in),
        out_specs=[far] * far_out + [held] * (len(outs) - far_out),
        scratch_shapes=scratch_shapes,
        cost_estimate=cost,
        compiler_params=pltpu.CompilerParams(vmem_limit_bytes=VMEM_BYTES),
    )(*[pltpu.with_memory_space_constraint(a, pltpu.HBM) for a in args[:far_in]], *args[far_in:])


def busy(bytes_accessed):
    return pl.CostEstimate(flops=0, bytes_accessed=bytes_accessed, transcendentals=0)


def swap_near(axis, face):
    return lax.ppermute(face, axis, [(i, i ^ 1) for i in range(lax.axis_size(axis))])


def swap_far(axis, face):
    size = lax.axis_size(axis)
    return lax.ppermute(face, axis, [(i, far_partner(i, size)) for i in range(size)])


def swap_all(x_near, x_far, y_near, y_far):
    y_far = swap_far("gy", y_far)
    x_far = swap_far("gx", x_far)
    x_near = swap_near("gx", x_near)
    y_near = swap_near("gy", y_near)
    return x_far, x_near, y_far, y_near


def far_partner(i, size):
    return (i + 1 if i % 2 else i - 1) % size


def partner_sum(values, axis, partners, riders):
    size, count = lax.axis_size(axis), values.shape[0]
    heard, faces = [], []
    for partner, rider in zip(partners, riders):
        load = values if rider is None else jnp.concatenate([values, rider])
        load = lax.ppermute(load, axis, [(i, partner(i)) for i in range(size)])
        heard.append(load[:count])
        if rider is not None:
            faces.append(load[count:])
    if len(heard) == 1:
        return values + heard[0], faces
    return (values + heard[0]) + (heard[1] + heard[2]), faces


def all_sum(values, axis, near, far):
    size = lax.axis_size(axis)
    half = size // 2

    def to_near(i):
        return i ^ 1

    def to_far(i):
        return far_partner(i, size)

    def across(i):
        return (i + half) % size

    def far_across(i):
        return across(to_far(i))

    if size == 4:
        values, (far, near) = partner_sum(values, axis, (to_far, to_near, across), (far, near, None))
        return values, near, far
    if size == 2:
        values, (far,) = partner_sum(values, axis, (to_far,), (far,))
        return values, lax.ppermute(near, axis, [(i, to_near(i)) for i in range(size)]), far
    values, (far,) = partner_sum(values, axis, (to_far, across, far_across), (far, None, None))
    values, (near,) = partner_sum(values, axis, (to_near,), (near,))
    bit = 4
    while bit < half:
        values, _ = partner_sum(values, axis, (lambda i, bit=bit: i ^ bit,), (None,))
        bit *= 2
    return values, near, far


def conjugate_coefficients(moments, centre, half):
    remaining, towards = list(moments), list(moments)
    one, zero = jnp.ones_like(moments[0]), jnp.zeros_like(moments[0])
    direction = [one] + [zero] * ITERS
    residual = list(direction)
    total = [zero] * ITERS
    for step in range(ITERS):
        count = len(towards) - 1
        image = []
        for level in range(count):
            side = (
                half * towards[1] if level == 0 else 0.5 * half * (towards[level + 1] + towards[level - 1])
            )
            image.append(centre * towards[level] + side)
        alpha = remaining[step] / image[step]
        total = [total[i] + alpha * direction[i] for i in range(ITERS)]
        if step == ITERS - 1:
            break
        applied = []
        for i in range(ITERS + 1):
            term = centre * direction[i]
            if i >= 1:
                term = term + (half if i == 1 else 0.5 * half) * direction[i - 1]
            if i < ITERS:
                term = term + 0.5 * half * direction[i + 1]
            applied.append(term)
        residual = [residual[i] - alpha * applied[i] for i in range(ITERS + 1)]
        following = [remaining[i] - alpha * image[i] for i in range(count)]
        beta = -alpha * (half if step == 0 else 0.5 * half) * following[step + 1] / remaining[step]
        towards = [following[i] + beta * towards[i] for i in range(count)]
        direction = [residual[i] + beta * direction[i] for i in range(ITERS + 1)]
        remaining = following
    return total


def on_device(old_fields, inverse_step, boundary):
    x, y, z = inverse_step.shape
    t = Tables(z)
    brick, four = (x, y, z), (4, x, y, z)
    faces = [(y, z)] * 2 + [(x, z)] * 2
    faces5 = [(5,) + f for f in faces]

    place = [lax.axis_index(a) % 2 == 0 for a in ("gx", "gy")]
    even = jnp.stack([jnp.full((8, 128), p, jnp.float32) for p in place])

    local, x_near, x_far, y_near, y_far = call(
        load_local, "local_right", [(5,) + brick] + faces5, old_fields, inverse_step, even,
        scratch=[four, brick], far_in=2, copies=5,
    )
    x_far = swap_far("gx", x_far)
    x_near = swap_near("gx", x_near)
    y_near, y_far = call(fix_corners, "corners", faces5[2:], y_near, y_far, x_near, x_far, even)
    y_far = swap_far("gy", y_far)
    y_near = swap_near("gy", y_near)

    top = INTERVAL_SHARE * np.array([spectrum_top(c) for c in DIFFUSE])
    halves = [float(v) for v in 0.5 * top]
    scales = [float(v) for v in np.array(DIFFUSE) / (0.5 * top)]
    rates = [float(v) for v in 1.0 / (0.5 * top)]

    received = (x_far, x_near, y_far, y_near)
    right, *sent = call(start_field, "right_field", [four] + faces5, local, boundary, *received, even)
    heard = [swap_all(*sent)]
    reaction, free, ahead, dots = call(
        functools.partial(start_sums, scales, rates), "right_sums", [brick, brick, four, (8, 128)],
        local, boundary, *received, even, right, t.summed, t.share, t.stiff_y, t.stiff_z, cost=busy(8 << 20),
    )
    basis, sums = [right], [dots]
    for k in range(1, ITERS - 1):
        here = scales if k == 1 else [2.0 * v for v in scales]
        field, *sent = call(
            functools.partial(grow_field, here), "basis_field", [four] + faces5,
            ahead, free, *heard[-1], even, t.summed,
        )
        heard.append(swap_all(*sent))
        ahead, dots = call(
            functools.partial(basis_sums, scales, rates), "basis_sums", [four, (8, 128)],
            field, basis[-1], reaction, free, t.summed, t.share, t.stiff_y, t.stiff_z, cost=busy(8 << 20),
        )
        basis.append(field)
        sums.append(dots)
    field, sums, x_near, x_far, y_near, y_far = call(
        functools.partial(last_field, scales, rates), "last_field", [four, (ITERS, 8, 128)] + faces,
        ahead, basis[-1], reaction, free, *heard[-1], even, t.summed, t.share, t.stiff_y, t.plain_z, t.local, *sums,
    )
    basis.append(field)
    sums = sums.reshape(ITERS * 8, z)
    sums, x_near, x_far = all_sum(sums, "gx", x_near, x_far)
    sums, y_near, y_far = all_sum(sums, "gy", y_near, y_far)
    sums = sums.reshape(ITERS, 8, z)
    slopes = (x_far, x_near, y_far, y_near)

    centre, half = chebyshev_bounds()
    factor = centre / half
    damping = 1.0 / factor
    fields, remainder, update, *sent = call(
        functools.partial(finish_fields, halves, 1.0 / centre), "fields", [four, brick, brick] + faces,
        sums, *basis, *[a for h in heard for a in h], *slopes, even, free, t.summed, t.slope_y, t.slope_z, t.inverse,
        scratch=[(ITERS, 8, 128), brick] + faces,
    )
    pressure = update
    for step in range(1, CHEB):
        last = step == CHEB - 1
        received = swap_all(*sent)
        (raw,) = call(
            pressure_sums, "pressure_sums", [brick],
            update, t.summed, t.shift, t.stiff_y, t.stiff_z, cost=busy(2 << 20),
        )
        following = 1.0 / (2.0 * factor - damping)
        keep, gain = following * damping, 2.0 * following / half
        damping = following
        kernel = functools.partial(pressure_step, last, keep, gain)
        args = [raw, free, *received, even, t.summed, t.inverse, remainder, update, pressure]
        if last:
            (pressure,) = call(
                kernel, "pressure_last", [brick], *args, scratch=[brick], far_out=1, copies=x // 8
            )
            break
        pressure, remainder, update, *sent = call(kernel, "pressure_step", [brick] * 3 + faces, *args)
    return (fields, pressure)


def solution(mesh):
    return jax.shard_map(
        on_device,
        mesh=mesh,
        in_specs=(P(None, "gx", "gy", None), P("gx", "gy", None), P("gx", "gy", None)),
        out_specs=(P(None, "gx", "gy", None), P("gx", "gy", None)),
        check_vma=False,
    )
```

profile of v0, /device:TPU:0, one launch (start us, length us, event | category | flops | bytes accessed | tf_op | source)
XLA Modules:
  0.0 109.9 jit_solution(13667777496796446422)
XLA Ops:
  0.7 2.0 %local_right.1 = (f32[5,32,16,128]{3,2,1,0:T(8,128)S(1)}, f32[5,16,128]{2,1,0:T(8,128)S(1)}, f32[5,16,128]{2,1,0:T(8,128)S(1)}, f32[5,32,128]{2,1,0:T(8,128)S(1)}, f32[5,32,128]{2,1,0:T(8,128)S(1)}) custom-call(f32[4,32,16,128]{3,2,1,0:T(8,128)} %old_far.1, f32[32,16,128]{2,1,0:T(8,128)} %step_far.1, f32[2,8,128]{2,1,0:T(8,128)S(1)} %stack.9.even_ref.refs_8_.refs_31_.refs_6_), custom_call_target="tpu_custom_call" | custom-call | tf_op jit(solution)/shard_map/local_right/pallas_call | solution.py:656
  2.8 4.0 %collective-permute-start = (f32[5,16,128]{2,1,0:T(8,128)S(1)}, f32[5,16,128]{2,1,0:T(8,128)S(1)}, u32[]{:S(2)}, u32[]{:S(2)}) collective-permute-start(f32[5,16,128]{2,1,0:T(8,128)S(1)} %get-tuple-element.88), channel_id=1, source_target_pairs={{0,24},{8,16},{16,8},{24,0},{1,25},{9,17},{17,9},{25,1},{2,26},{10... | collective-permute-start | bytes 122888 | tf_op jit(solution)/shard_map/ppermute | solution.py:678
  7.3 1.4 %collective-permute-done.x_far = f32[5,16,128]{2,1,0:T(8,128)S(1)} collective-permute-done((f32[5,16,128]{2,1,0:T(8,128)S(1)}, f32[5,16,128]{2,1,0:T(8,128)S(1)}, u32[]{:S(2)}, u32[]{:S(2)}) %collective-permute-start) | collective-permute-done | bytes 40992 | tf_op jit(solution)/shard_map/ppermute | solution.py:678
  8.7 2.0 %collective-permute-done.1.x_near = f32[5,16,128]{2,1,0:T(8,128)S(1)} collective-permute-done((f32[5,16,128]{2,1,0:T(8,128)S(1)}, f32[5,16,128]{2,1,0:T(8,128)S(1)}, u32[]{:S(2)}, u32[]{:S(2)}) %collective-permute-start.1) | collective-permute-done | bytes 40992 | tf_op jit(solution)/shard_map/ppermute | solution.py:673
  10.8 2.2 %collective-permute-start.2 = (f32[5,32,128]{2,1,0:T(8,128)S(1)}, f32[5,32,128]{2,1,0:T(8,128)S(1)}, u32[]{:S(2)}, u32[]{:S(2)}) collective-permute-start(f32[5,32,128]{2,1,0:T(8,128)S(1)} %get-tuple-element.92), channel_id=1, source_target_pairs={{0,7},{1,2},{2,1},{3,4},{4,3},{5,6},{6,5},{7,0},{8,15},{9,10},{10,... | collective-permute-start | bytes 245768 | tf_op jit(solution)/shard_map/ppermute | solution.py:678
  13.0 4.1 %collective-permute-done.2.y_far = f32[5,32,128]{2,1,0:T(8,128)S(1)} collective-permute-done((f32[5,32,128]{2,1,0:T(8,128)S(1)}, f32[5,32,128]{2,1,0:T(8,128)S(1)}, u32[]{:S(2)}, u32[]{:S(2)}) %collective-permute-start.2) | collective-permute-done | bytes 81952 | tf_op jit(solution)/shard_map/ppermute | solution.py:678
  17.8 1.6 %collective-permute-start.6 = (f32[5,32,128]{2,1,0:T(8,128)S(1)}, f32[5,32,128]{2,1,0:T(8,128)S(1)}, u32[]{:S(2)}, u32[]{:S(2)}) collective-permute-start(f32[5,32,128]{2,1,0:T(8,128)S(1)} %get-tuple-element.99), channel_id=1, source_target_pairs={{0,7},{1,2},{2,1},{3,4},{4,3},{5,6},{6,5},{7,0},{8,15},{9,10},{10,... | collective-permute-start | bytes 245768 | tf_op jit(solution)/shard_map/ppermute | solution.py:678
  21.3 2.6 %right_sums.1 = (f32[32,16,128]{2,1,0:T(8,128)S(1)}, f32[32,16,128]{2,1,0:T(8,128)S(1)}, f32[4,32,16,128]{3,2,1,0:T(8,128)S(1)}, f32[8,128]{1,0:T(8,128)S(1)}) custom-call(f32[5,32,16,128]{3,2,1,0:T(8,128)S(1)} %get-tuple-element.87.local, s32[32,16,128]{2,1,0:T(8,128)S(1)} %copy-done.5, f32[5,16,128]{2,1,0:T(8,128)S(1)} %collective-permute-done.x_far, ...), custom_call_target="tpu_custom_call" | custom-call | bytes 8388608 | tf_op jit(solution)/shard_map/right_sums/pallas_call | solution.py:656
  26.1 2.0 %collective-permute-start.8 = (f32[5,16,128]{2,1,0:T(8,128)S(1)}, f32[5,16,128]{2,1,0:T(8,128)S(1)}, u32[]{:S(2)}, u32[]{:S(2)}) collective-permute-start(f32[5,16,128]{2,1,0:T(8,128)S(1)} %get-tuple-element.104), channel_id=1, source_target_pairs={{0,24},{8,16},{16,8},{24,0},{1,25},{9,17},{17,9},{25,1},{2,26},{10... | collective-permute-start | bytes 122888 | tf_op jit(solution)/shard_map/ppermute | solution.py:678
  29.1 2.6 %basis_sums.4 = (f32[4,32,16,128]{3,2,1,0:T(8,128)S(1)}, f32[8,128]{1,0:T(8,128)S(1)}) custom-call(f32[4,32,16,128]{3,2,1,0:T(8,128)S(1)} %get-tuple-element.101.newest.older.refs_2_, f32[4,32,16,128]{3,2,1,0:T(8,128)S(1)} %get-tuple-element.94.right.older.refs_1_, f32[32,16,128]{2,1,0:T(8,128)S(1)} %get-tuple-element.102.reaction.refs_2_, ...), custom_call_target="tpu_custom_call" | custom-call | bytes 8388608 | tf_op jit(solution)/shard_map/basis_sums/pallas_call | solution.py:656
  32.8 1.8 %collective-permute-start.14 = (f32[5,32,128]{2,1,0:T(8,128)S(1)}, f32[5,32,128]{2,1,0:T(8,128)S(1)}, u32[]{:S(2)}, u32[]{:S(2)}) collective-permute-start(f32[5,32,128]{2,1,0:T(8,128)S(1)} %get-tuple-element.112), channel_id=1, source_target_pairs={{0,7},{1,2},{2,1},{3,4},{4,3},{5,6},{6,5},{7,0},{8,15},{9,10},{10,... | collective-permute-start | bytes 245768 | tf_op jit(solution)/shard_map/ppermute | solution.py:678
  36.7 2.6 %basis_sums.5 = (f32[4,32,16,128]{3,2,1,0:T(8,128)S(1)}, f32[8,128]{1,0:T(8,128)S(1)}) custom-call(f32[4,32,16,128]{3,2,1,0:T(8,128)S(1)} %get-tuple-element.108.newest.older.refs_3_, f32[4,32,16,128]{3,2,1,0:T(8,128)S(1)} %get-tuple-element.101.newest.older.refs_2_, f32[32,16,128]{2,1,0:T(8,128)S(1)} %get-tuple-element.102.reaction.refs_2_, ...), custom_call_target="tpu_custom_call" | custom-call | bytes 8388608 | tf_op jit(solution)/shard_map/basis_sums/pallas_call | solution.py:656
  41.3 2.0 %collective-permute-start.16 = (f32[5,16,128]{2,1,0:T(8,128)S(1)}, f32[5,16,128]{2,1,0:T(8,128)S(1)}, u32[]{:S(2)}, u32[]{:S(2)}) collective-permute-start(f32[5,16,128]{2,1,0:T(8,128)S(1)} %get-tuple-element.116), channel_id=1, source_target_pairs={{0,24},{8,16},{16,8},{24,0},{1,25},{9,17},{17,9},{25,1},{2,26},{10... | collective-permute-start | bytes 122888 | tf_op jit(solution)/shard_map/ppermute | solution.py:678
  44.1 2.5 %basis_sums.6 = (f32[4,32,16,128]{3,2,1,0:T(8,128)S(1)}, f32[8,128]{1,0:T(8,128)S(1)}) custom-call(f32[4,32,16,128]{3,2,1,0:T(8,128)S(1)} %get-tuple-element.114.newest.older.refs_4_, f32[4,32,16,128]{3,2,1,0:T(8,128)S(1)} %get-tuple-element.108.newest.older.refs_3_, f32[32,16,128]{2,1,0:T(8,128)S(1)} %get-tuple-element.102.reaction.refs_2_, ...), custom_call_target="tpu_custom_call" | custom-call | bytes 8388608 | tf_op jit(solution)/shard_map/basis_sums/pallas_call | solution.py:656
  48.0 1.7 %collective-permute-start.22 = (f32[5,32,128]{2,1,0:T(8,128)S(1)}, f32[5,32,128]{2,1,0:T(8,128)S(1)}, u32[]{:S(2)}, u32[]{:S(2)}) collective-permute-start(f32[5,32,128]{2,1,0:T(8,128)S(1)} %get-tuple-element.124), channel_id=1, source_target_pairs={{0,7},{1,2},{2,1},{3,4},{4,3},{5,6},{6,5},{7,0},{8,15},{9,10},{10,... | collective-permute-start | bytes 245768 | tf_op jit(solution)/shard_map/ppermute | solution.py:678
  51.8 2.5 %basis_sums.7 = (f32[4,32,16,128]{3,2,1,0:T(8,128)S(1)}, f32[8,128]{1,0:T(8,128)S(1)}) custom-call(f32[4,32,16,128]{3,2,1,0:T(8,128)S(1)} %get-tuple-element.120.newest.refs_1_.refs_5_, f32[4,32,16,128]{3,2,1,0:T(8,128)S(1)} %get-tuple-element.114.newest.older.refs_4_, f32[32,16,128]{2,1,0:T(8,128)S(1)} %get-tuple-element.102.reaction.refs_2_, ...), custom_call_target="tpu_custom_call" | custom-call | bytes 8388608 | tf_op jit(solution)/shard_map/basis_sums/pallas_call | solution.py:656
  55.0 2.6 %last_field.1 = (f32[4,32,16,128]{3,2,1,0:T(8,128)S(1)}, f32[6,8,128]{2,1,0:T(8,128)S(1)}, f32[16,128]{1,0:T(8,128)S(1)}, f32[16,128]{1,0:T(8,128)S(1)}, f32[32,128]{1,0:T(8,128)S(1)}, /*index=5*/f32[32,128]{1,0:T(8,128)S(1)}) custom-call(f32[4,32,16,128]{3,2,1,0:T(8,128)S(1)} %get-tuple-element.121.refs_0_, ...), custom_call_target="tpu_custom_call" | custom-call | tf_op jit(solution)/shard_map/last_field/pallas_call | solution.py:656
  57.7 1.7 %collective-permute-start.24 = (f32[64,128]{1,0:T(8,128)S(1)}, f32[64,128]{1,0:T(8,128)S(1)}, u32[]{:S(2)}, u32[]{:S(2)}) collective-permute-start(f32[64,128]{1,0:T(8,128)S(1)} %get-tuple-element.172), channel_id=1, source_target_pairs={{0,24},{8,16},{16,8},{24,0},{1,25},{9,17},{17,9},{25,1},{2,26},{10... | collective-permute-start | bytes 98312 | tf_op jit(solution)/shard_map/ppermute | solution.py:698
  61.2 2.9 %collective-permute-done.26 = f32[48,128]{1,0:T(8,128)S(1)} collective-permute-done((f32[48,128]{1,0:T(8,128)S(1)}, f32[48,128]{1,0:T(8,128)S(1)}, u32[]{:S(2)}, u32[]{:S(2)}) %collective-permute-start.26) | collective-permute-done | bytes 24608 | tf_op jit(solution)/shard_map/ppermute | solution.py:698
  64.2 2.1 %collective-permute-start.29 = (f32[48,128]{1,0:T(8,128)S(1)}, f32[48,128]{1,0:T(8,128)S(1)}, u32[]{:S(2)}, u32[]{:S(2)}) collective-permute-start(f32[48,128]{1,0:T(8,128)S(1)} %fusion.2), channel_id=1, source_target_pairs={{0,3},{1,6},{2,5},{3,0},{4,7},{5,2},{6,1},{7,4},{8,11},{9,14},{10,... | collective-permute-start | bytes 73736 | tf_op jit(solution)/shard_map/ppermute | solution.py:698
  66.4 2.0 %collective-permute-start.28 = (f32[48,128]{1,0:T(8,128)S(1)}, f32[48,128]{1,0:T(8,128)S(1)}, u32[]{:S(2)}, u32[]{:S(2)}) collective-permute-start(f32[48,128]{1,0:T(8,128)S(1)} %fusion.2), channel_id=1, source_target_pairs={{0,4},{1,5},{2,6},{3,7},{4,0},{5,1},{6,2},{7,3},{8,12},{9,13},{10,... | collective-permute-start | bytes 73736 | tf_op jit(solution)/shard_map/ppermute | solution.py:698
  68.3 2.8 %collective-permute-done.28 = f32[48,128]{1,0:T(8,128)S(1)} collective-permute-done((f32[48,128]{1,0:T(8,128)S(1)}, f32[48,128]{1,0:T(8,128)S(1)}, u32[]{:S(2)}, u32[]{:S(2)}) %collective-permute-start.28) | collective-permute-done | bytes 24608 | tf_op jit(solution)/shard_map/ppermute | solution.py:698
  72.5 2.5 %fields.1 = (f32[4,32,16,128]{3,2,1,0:T(8,128)}, f32[32,16,128]{2,1,0:T(8,128)S(1)}, f32[32,16,128]{2,1,0:T(8,128)S(1)}, f32[16,128]{1,0:T(8,128)S(1)}, f32[16,1...) custom-call(f32[6,8,128]{2,1,0:T(8,128)S(1)} %fusion.refs_0_, ...), custom_call_target="tpu_custom_call" | custom-call | tf_op jit(solution)/shard_map/fields/pallas_call | solution.py:656
  75.0 2.1 %collective-permute-start.33 = (f32[32,128]{1,0:T(8,128)S(1)}, f32[32,128]{1,0:T(8,128)S(1)}, u32[]{:S(2)}, u32[]{:S(2)}) collective-permute-start(f32[32,128]{1,0:T(8,128)S(1)} %get-tuple-element.141), channel_id=1, source_target_pairs={{0,7},{1,2},{2,1},{3,4},{4,3},{5,6},{6,5},{7,0},{8,15},{9,10},{10,... | collective-permute-start | bytes 49160 | tf_op jit(solution)/shard_map/ppermute | solution.py:678
  79.8 1.9 %collective-permute-done.31.refs_2_ = f32[16,128]{1,0:T(8,128)S(1)} collective-permute-done((f32[16,128]{1,0:T(8,128)S(1)}, f32[16,128]{1,0:T(8,128)S(1)}, u32[]{:S(2)}, u32[]{:S(2)}) %collective-permute-start.31) | collective-permute-done | bytes 8224 | tf_op jit(solution)/shard_map/ppermute | solution.py:678
  82.8 1.7 %collective-permute-start.35 = (f32[16,128]{1,0:T(8,128)S(1)}, f32[16,128]{1,0:T(8,128)S(1)}, u32[]{:S(2)}, u32[]{:S(2)}) collective-permute-start(f32[16,128]{1,0:T(8,128)S(1)} %get-tuple-element.145), channel_id=1, source_target_pairs={{0,24},{8,16},{16,8},{24,0},{1,25},{9,17},{17,9},{25,1},{2,26},{10... | collective-permute-start | bytes 24584 | tf_op jit(solution)/shard_map/ppermute | solution.py:678
  88.5 1.9 %collective-permute-start.41 = (f32[32,128]{1,0:T(8,128)S(1)}, f32[32,128]{1,0:T(8,128)S(1)}, u32[]{:S(2)}, u32[]{:S(2)}) collective-permute-start(f32[32,128]{1,0:T(8,128)S(1)} %get-tuple-element.154), channel_id=1, source_target_pairs={{0,7},{1,2},{2,1},{3,4},{4,3},{5,6},{6,5},{7,0},{8,15},{9,10},{10,... | collective-permute-start | bytes 49160 | tf_op jit(solution)/shard_map/ppermute | solution.py:678
  92.8 2.1 %collective-permute-done.39.refs_2_ = f32[16,128]{1,0:T(8,128)S(1)} collective-permute-done((f32[16,128]{1,0:T(8,128)S(1)}, f32[16,128]{1,0:T(8,128)S(1)}, u32[]{:S(2)}, u32[]{:S(2)}) %collective-permute-start.39) | collective-permute-done | bytes 8224 | tf_op jit(solution)/shard_map/ppermute | solution.py:678
  96.4 1.7 %collective-permute-start.43 = (f32[16,128]{1,0:T(8,128)S(1)}, f32[16,128]{1,0:T(8,128)S(1)}, u32[]{:S(2)}, u32[]{:S(2)}) collective-permute-start(f32[16,128]{1,0:T(8,128)S(1)} %get-tuple-element.159), channel_id=1, source_target_pairs={{0,24},{8,16},{16,8},{24,0},{1,25},{9,17},{17,9},{25,1},{2,26},{10... | collective-permute-start | bytes 24584 | tf_op jit(solution)/shard_map/ppermute | solution.py:678
  99.8 1.2 %collective-permute-done.43.refs_2_ = f32[16,128]{1,0:T(8,128)S(1)} collective-permute-done((f32[16,128]{1,0:T(8,128)S(1)}, f32[16,128]{1,0:T(8,128)S(1)}, u32[]{:S(2)}, u32[]{:S(2)}) %collective-permute-start.43) | collective-permute-done | bytes 8224 | tf_op jit(solution)/shard_map/ppermute | solution.py:678
  102.0 1.6 %collective-permute-start.49 = (f32[32,128]{1,0:T(8,128)S(1)}, f32[32,128]{1,0:T(8,128)S(1)}, u32[]{:S(2)}, u32[]{:S(2)}) collective-permute-start(f32[32,128]{1,0:T(8,128)S(1)} %get-tuple-element.168), channel_id=1, source_target_pairs={{0,7},{1,2},{2,1},{3,4},{4,3},{5,6},{6,5},{7,0},{8,15},{9,10},{10,... | collective-permute-start | bytes 49160 | tf_op jit(solution)/shard_map/ppermute | solution.py:678
  106.8 1.9 %collective-permute-done.47.refs_2_ = f32[16,128]{1,0:T(8,128)S(1)} collective-permute-done((f32[16,128]{1,0:T(8,128)S(1)}, f32[16,128]{1,0:T(8,128)S(1)}, u32[]{:S(2)}, u32[]{:S(2)}) %collective-permute-start.47) | collective-permute-done | bytes 8224 | tf_op jit(solution)/shard_map/ppermute | solution.py:678
  (128 shorter events, 38.5 us)
Async XLA Ops:
  2.8 5.9 %collective-permute-start = (f32[5,16,128]{2,1,0:T(8,128)S(1)}, f32[5,16,128]{2,1,0:T(8,128)S(1)}, u32[]{:S(2)}, u32[]{:S(2)}) collective-permute-start(f32[5,16,128]{2,1,0:T(8,128)S(1)} %get-tuple-element.88), channel_id=1, source_target_pairs={{0,24},{8,16},{16,8},{24,0},{1,25},{9,17},{17,9},{25,1},{2,26},{10... | collective-permute-start | bytes 122888 | tf_op jit(solution)/shard_map/ppermute | solution.py:678
  10.8 6.3 %collective-permute-start.2 = (f32[5,32,128]{2,1,0:T(8,128)S(1)}, f32[5,32,128]{2,1,0:T(8,128)S(1)}, u32[]{:S(2)}, u32[]{:S(2)}) collective-permute-start(f32[5,32,128]{2,1,0:T(8,128)S(1)} %get-tuple-element.92), channel_id=1, source_target_pairs={{0,7},{1,2},{2,1},{3,4},{4,3},{5,6},{6,5},{7,0},{8,15},{9,10},{10,... | collective-permute-start | bytes 245768 | tf_op jit(solution)/shard_map/ppermute | solution.py:678
  17.8 6.9 %collective-permute-start.6 = (f32[5,32,128]{2,1,0:T(8,128)S(1)}, f32[5,32,128]{2,1,0:T(8,128)S(1)}, u32[]{:S(2)}, u32[]{:S(2)}) collective-permute-start(f32[5,32,128]{2,1,0:T(8,128)S(1)} %get-tuple-element.99), channel_id=1, source_target_pairs={{0,7},{1,2},{2,1},{3,4},{4,3},{5,6},{6,5},{7,0},{8,15},{9,10},{10,... | collective-permute-start | bytes 245768 | tf_op jit(solution)/shard_map/ppermute | solution.py:678
  19.4 5.3 %collective-permute-start.7 = (f32[5,32,128]{2,1,0:T(8,128)S(1)}, f32[5,32,128]{2,1,0:T(8,128)S(1)}, u32[]{:S(2)}, u32[]{:S(2)}) collective-permute-start(f32[5,32,128]{2,1,0:T(8,128)S(1)} %get-tuple-element.100), channel_id=1, source_target_pairs={{0,1},{1,0},{2,3},{3,2},{4,5},{5,4},{6,7},{7,6},{8,9},{9,8},{10,11... | collective-permute-start | bytes 245768 | tf_op jit(solution)/shard_map/ppermute | solution.py:673
  19.4 5.3 %collective-permute-start.4 = (f32[5,16,128]{2,1,0:T(8,128)S(1)}, f32[5,16,128]{2,1,0:T(8,128)S(1)}, u32[]{:S(2)}, u32[]{:S(2)}) collective-permute-start(f32[5,16,128]{2,1,0:T(8,128)S(1)} %get-tuple-element.97), channel_id=1, source_target_pairs={{0,24},{8,16},{16,8},{24,0},{1,25},{9,17},{17,9},{25,1},{2,26},{10... | collective-permute-start | bytes 122888 | tf_op jit(solution)/shard_map/ppermute | solution.py:678
  25.3 6.8 %collective-permute-start.10 = (f32[5,32,128]{2,1,0:T(8,128)S(1)}, f32[5,32,128]{2,1,0:T(8,128)S(1)}, u32[]{:S(2)}, u32[]{:S(2)}) collective-permute-start(f32[5,32,128]{2,1,0:T(8,128)S(1)} %get-tuple-element.106), channel_id=1, source_target_pairs={{0,7},{1,2},{2,1},{3,4},{4,3},{5,6},{6,5},{7,0},{8,15},{9,10},{10,... | collective-permute-start | bytes 245768 | tf_op jit(solution)/shard_map/ppermute | solution.py:678
  26.1 6.0 %collective-permute-start.11 = (f32[5,32,128]{2,1,0:T(8,128)S(1)}, f32[5,32,128]{2,1,0:T(8,128)S(1)}, u32[]{:S(2)}, u32[]{:S(2)}) collective-permute-start(f32[5,32,128]{2,1,0:T(8,128)S(1)} %get-tuple-element.107), channel_id=1, source_target_pairs={{0,1},{1,0},{2,3},{3,2},{4,5},{5,4},{6,7},{7,6},{8,9},{9,8},{10,11... | collective-permute-start | bytes 245768 | tf_op jit(solution)/shard_map/ppermute | solution.py:673
  26.1 5.6 %collective-permute-start.8 = (f32[5,16,128]{2,1,0:T(8,128)S(1)}, f32[5,16,128]{2,1,0:T(8,128)S(1)}, u32[]{:S(2)}, u32[]{:S(2)}) collective-permute-start(f32[5,16,128]{2,1,0:T(8,128)S(1)} %get-tuple-element.104), channel_id=1, source_target_pairs={{0,24},{8,16},{16,8},{24,0},{1,25},{9,17},{17,9},{25,1},{2,26},{10... | collective-permute-start | bytes 122888 | tf_op jit(solution)/shard_map/ppermute | solution.py:678
  32.8 7.0 %collective-permute-start.14 = (f32[5,32,128]{2,1,0:T(8,128)S(1)}, f32[5,32,128]{2,1,0:T(8,128)S(1)}, u32[]{:S(2)}, u32[]{:S(2)}) collective-permute-start(f32[5,32,128]{2,1,0:T(8,128)S(1)} %get-tuple-element.112), channel_id=1, source_target_pairs={{0,7},{1,2},{2,1},{3,4},{4,3},{5,6},{6,5},{7,0},{8,15},{9,10},{10,... | collective-permute-start | bytes 245768 | tf_op jit(solution)/shard_map/ppermute | solution.py:678
  34.5 5.2 %collective-permute-start.15 = (f32[5,32,128]{2,1,0:T(8,128)S(1)}, f32[5,32,128]{2,1,0:T(8,128)S(1)}, u32[]{:S(2)}, u32[]{:S(2)}) collective-permute-start(f32[5,32,128]{2,1,0:T(8,128)S(1)} %get-tuple-element.113), channel_id=1, source_target_pairs={{0,1},{1,0},{2,3},{3,2},{4,5},{5,4},{6,7},{7,6},{8,9},{9,8},{10,11... | collective-permute-start | bytes 245768 | tf_op jit(solution)/shard_map/ppermute | solution.py:673
  34.5 5.2 %collective-permute-start.12 = (f32[5,16,128]{2,1,0:T(8,128)S(1)}, f32[5,16,128]{2,1,0:T(8,128)S(1)}, u32[]{:S(2)}, u32[]{:S(2)}) collective-permute-start(f32[5,16,128]{2,1,0:T(8,128)S(1)} %get-tuple-element.110), channel_id=1, source_target_pairs={{0,24},{8,16},{16,8},{24,0},{1,25},{9,17},{17,9},{25,1},{2,26},{10... | collective-permute-start | bytes 122888 | tf_op jit(solution)/shard_map/ppermute | solution.py:678
  40.5 6.9 %collective-permute-start.18 = (f32[5,32,128]{2,1,0:T(8,128)S(1)}, f32[5,32,128]{2,1,0:T(8,128)S(1)}, u32[]{:S(2)}, u32[]{:S(2)}) collective-permute-start(f32[5,32,128]{2,1,0:T(8,128)S(1)} %get-tuple-element.118), channel_id=1, source_target_pairs={{0,7},{1,2},{2,1},{3,4},{4,3},{5,6},{6,5},{7,0},{8,15},{9,10},{10,... | collective-permute-start | bytes 245768 | tf_op jit(solution)/shard_map/ppermute | solution.py:678
  41.3 6.1 %collective-permute-start.19 = (f32[5,32,128]{2,1,0:T(8,128)S(1)}, f32[5,32,128]{2,1,0:T(8,128)S(1)}, u32[]{:S(2)}, u32[]{:S(2)}) collective-permute-start(f32[5,32,128]{2,1,0:T(8,128)S(1)} %get-tuple-element.119), channel_id=1, source_target_pairs={{0,1},{1,0},{2,3},{3,2},{4,5},{5,4},{6,7},{7,6},{8,9},{9,8},{10,11... | collective-permute-start | bytes 245768 | tf_op jit(solution)/shard_map/ppermute | solution.py:673
  41.3 5.4 %collective-permute-start.16 = (f32[5,16,128]{2,1,0:T(8,128)S(1)}, f32[5,16,128]{2,1,0:T(8,128)S(1)}, u32[]{:S(2)}, u32[]{:S(2)}) collective-permute-start(f32[5,16,128]{2,1,0:T(8,128)S(1)} %get-tuple-element.116), channel_id=1, source_target_pairs={{0,24},{8,16},{16,8},{24,0},{1,25},{9,17},{17,9},{25,1},{2,26},{10... | collective-permute-start | bytes 122888 | tf_op jit(solution)/shard_map/ppermute | solution.py:678
  48.0 7.0 %collective-permute-start.22 = (f32[5,32,128]{2,1,0:T(8,128)S(1)}, f32[5,32,128]{2,1,0:T(8,128)S(1)}, u32[]{:S(2)}, u32[]{:S(2)}) collective-permute-start(f32[5,32,128]{2,1,0:T(8,128)S(1)} %get-tuple-element.124), channel_id=1, source_target_pairs={{0,7},{1,2},{2,1},{3,4},{4,3},{5,6},{6,5},{7,0},{8,15},{9,10},{10,... | collective-permute-start | bytes 245768 | tf_op jit(solution)/shard_map/ppermute | solution.py:678
  49.7 5.3 %collective-permute-start.23 = (f32[5,32,128]{2,1,0:T(8,128)S(1)}, f32[5,32,128]{2,1,0:T(8,128)S(1)}, u32[]{:S(2)}, u32[]{:S(2)}) collective-permute-start(f32[5,32,128]{2,1,0:T(8,128)S(1)} %get-tuple-element.125), channel_id=1, source_target_pairs={{0,1},{1,0},{2,3},{3,2},{4,5},{5,4},{6,7},{7,6},{8,9},{9,8},{10,11... | collective-permute-start | bytes 245768 | tf_op jit(solution)/shard_map/ppermute | solution.py:673
  49.7 5.3 %collective-permute-start.20 = (f32[5,16,128]{2,1,0:T(8,128)S(1)}, f32[5,16,128]{2,1,0:T(8,128)S(1)}, u32[]{:S(2)}, u32[]{:S(2)}) collective-permute-start(f32[5,16,128]{2,1,0:T(8,128)S(1)} %get-tuple-element.122), channel_id=1, source_target_pairs={{0,24},{8,16},{16,8},{24,0},{1,25},{9,17},{17,9},{25,1},{2,26},{10... | collective-permute-start | bytes 122888 | tf_op jit(solution)/shard_map/ppermute | solution.py:678
  57.7 6.4 %collective-permute-start.24 = (f32[64,128]{1,0:T(8,128)S(1)}, f32[64,128]{1,0:T(8,128)S(1)}, u32[]{:S(2)}, u32[]{:S(2)}) collective-permute-start(f32[64,128]{1,0:T(8,128)S(1)} %get-tuple-element.172), channel_id=1, source_target_pairs={{0,24},{8,16},{16,8},{24,0},{1,25},{9,17},{17,9},{25,1},{2,26},{10... | collective-permute-start | bytes 98312 | tf_op jit(solution)/shard_map/ppermute | solution.py:698
  59.4 4.7 %collective-permute-start.25 = (f32[64,128]{1,0:T(8,128)S(1)}, f32[64,128]{1,0:T(8,128)S(1)}, u32[]{:S(2)}, u32[]{:S(2)}) collective-permute-start(f32[64,128]{1,0:T(8,128)S(1)} %get-tuple-element.173), channel_id=1, source_target_pairs={{0,8},{8,0},{16,24},{24,16},{1,9},{9,1},{17,25},{25,17},{2,10},{10... | collective-permute-start | bytes 98312 | tf_op jit(solution)/shard_map/ppermute | solution.py:698
  64.1 6.9 %collective-permute-start.27 = (f32[80,128]{1,0:T(8,128)S(1)}, f32[80,128]{1,0:T(8,128)S(1)}, u32[]{:S(2)}, u32[]{:S(2)}) collective-permute-start(f32[80,128]{1,0:T(8,128)S(1)} %pad_maximum_fusion), channel_id=1, source_target_pairs={{0,7},{1,2},{2,1},{3,4},{4,3},{5,6},{6,5},{7,0},{8,15},{9,10},{10,... | collective-permute-start | bytes 122888 | tf_op jit(solution)/shard_map/ppermute | solution.py:698
  66.4 4.7 %collective-permute-start.28 = (f32[48,128]{1,0:T(8,128)S(1)}, f32[48,128]{1,0:T(8,128)S(1)}, u32[]{:S(2)}, u32[]{:S(2)}) collective-permute-start(f32[48,128]{1,0:T(8,128)S(1)} %fusion.2), channel_id=1, source_target_pairs={{0,4},{1,5},{2,6},{3,7},{4,0},{5,1},{6,2},{7,3},{8,12},{9,13},{10,... | collective-permute-start | bytes 73736 | tf_op jit(solution)/shard_map/ppermute | solution.py:698
  75.0 6.9 %collective-permute-start.33 = (f32[32,128]{1,0:T(8,128)S(1)}, f32[32,128]{1,0:T(8,128)S(1)}, u32[]{:S(2)}, u32[]{:S(2)}) collective-permute-start(f32[32,128]{1,0:T(8,128)S(1)} %get-tuple-element.141), channel_id=1, source_target_pairs={{0,7},{1,2},{2,1},{3,4},{4,3},{5,6},{6,5},{7,0},{8,15},{9,10},{10,... | collective-permute-start | bytes 49160 | tf_op jit(solution)/shard_map/ppermute | solution.py:678
  77.1 4.8 %collective-permute-start.34 = (f32[32,128]{1,0:T(8,128)S(1)}, f32[32,128]{1,0:T(8,128)S(1)}, u32[]{:S(2)}, u32[]{:S(2)}) collective-permute-start(f32[32,128]{1,0:T(8,128)S(1)} %get-tuple-element.142), channel_id=1, source_target_pairs={{0,1},{1,0},{2,3},{3,2},{4,5},{5,4},{6,7},{7,6},{8,9},{9,8},{10,11... | collective-permute-start | bytes 49160 | tf_op jit(solution)/shard_map/ppermute | solution.py:673
  82.1 6.1 %collective-permute-start.37 = (f32[32,128]{1,0:T(8,128)S(1)}, f32[32,128]{1,0:T(8,128)S(1)}, u32[]{:S(2)}, u32[]{:S(2)}) collective-permute-start(f32[32,128]{1,0:T(8,128)S(1)} %get-tuple-element.147), channel_id=1, source_target_pairs={{0,7},{1,2},{2,1},{3,4},{4,3},{5,6},{6,5},{7,0},{8,15},{9,10},{10,... | collective-permute-start | bytes 49160 | tf_op jit(solution)/shard_map/ppermute | solution.py:678
  82.3 5.9 %collective-permute-start.38 = (f32[32,128]{1,0:T(8,128)S(1)}, f32[32,128]{1,0:T(8,128)S(1)}, u32[]{:S(2)}, u32[]{:S(2)}) collective-permute-start(f32[32,128]{1,0:T(8,128)S(1)} %get-tuple-element.148), channel_id=1, source_target_pairs={{0,1},{1,0},{2,3},{3,2},{4,5},{5,4},{6,7},{7,6},{8,9},{9,8},{10,11... | collective-permute-start | bytes 49160 | tf_op jit(solution)/shard_map/ppermute | solution.py:673
  82.8 4.6 %collective-permute-start.35 = (f32[16,128]{1,0:T(8,128)S(1)}, f32[16,128]{1,0:T(8,128)S(1)}, u32[]{:S(2)}, u32[]{:S(2)}) collective-permute-start(f32[16,128]{1,0:T(8,128)S(1)} %get-tuple-element.145), channel_id=1, source_target_pairs={{0,24},{8,16},{16,8},{24,0},{1,25},{9,17},{17,9},{25,1},{2,26},{10... | collective-permute-start | bytes 24584 | tf_op jit(solution)/shard_map/ppermute | solution.py:678
  88.5 6.4 %collective-permute-start.41 = (f32[32,128]{1,0:T(8,128)S(1)}, f32[32,128]{1,0:T(8,128)S(1)}, u32[]{:S(2)}, u32[]{:S(2)}) collective-permute-start(f32[32,128]{1,0:T(8,128)S(1)} %get-tuple-element.154), channel_id=1, source_target_pairs={{0,7},{1,2},{2,1},{3,4},{4,3},{5,6},{6,5},{7,0},{8,15},{9,10},{10,... | collective-permute-start | bytes 49160 | tf_op jit(solution)/shard_map/ppermute | solution.py:678
  95.1 6.6 %collective-permute-start.45 = (f32[32,128]{1,0:T(8,128)S(1)}, f32[32,128]{1,0:T(8,128)S(1)}, u32[]{:S(2)}, u32[]{:S(2)}) collective-permute-start(f32[32,128]{1,0:T(8,128)S(1)} %get-tuple-element.161), channel_id=1, source_target_pairs={{0,7},{1,2},{2,1},{3,4},{4,3},{5,6},{6,5},{7,0},{8,15},{9,10},{10,... | collective-permute-start | bytes 49160 | tf_op jit(solution)/shard_map/ppermute | solution.py:678
  95.8 5.9 %collective-permute-start.46 = (f32[32,128]{1,0:T(8,128)S(1)}, f32[32,128]{1,0:T(8,128)S(1)}, u32[]{:S(2)}, u32[]{:S(2)}) collective-permute-start(f32[32,128]{1,0:T(8,128)S(1)} %get-tuple-element.162), channel_id=1, source_target_pairs={{0,1},{1,0},{2,3},{3,2},{4,5},{5,4},{6,7},{7,6},{8,9},{9,8},{10,11... | collective-permute-start | bytes 49160 | tf_op jit(solution)/shard_map/ppermute | solution.py:673
  96.4 4.6 %collective-permute-start.43 = (f32[16,128]{1,0:T(8,128)S(1)}, f32[16,128]{1,0:T(8,128)S(1)}, u32[]{:S(2)}, u32[]{:S(2)}) collective-permute-start(f32[16,128]{1,0:T(8,128)S(1)} %get-tuple-element.159), channel_id=1, source_target_pairs={{0,24},{8,16},{16,8},{24,0},{1,25},{9,17},{17,9},{25,1},{2,26},{10... | collective-permute-start | bytes 24584 | tf_op jit(solution)/shard_map/ppermute | solution.py:678
  102.0 7.0 %collective-permute-start.49 = (f32[32,128]{1,0:T(8,128)S(1)}, f32[32,128]{1,0:T(8,128)S(1)}, u32[]{:S(2)}, u32[]{:S(2)}) collective-permute-start(f32[32,128]{1,0:T(8,128)S(1)} %get-tuple-element.168), channel_id=1, source_target_pairs={{0,7},{1,2},{2,1},{3,4},{4,3},{5,6},{6,5},{7,0},{8,15},{9,10},{10,... | collective-permute-start | bytes 49160 | tf_op jit(solution)/shard_map/ppermute | solution.py:678
  103.6 5.4 %collective-permute-start.50 = (f32[32,128]{1,0:T(8,128)S(1)}, f32[32,128]{1,0:T(8,128)S(1)}, u32[]{:S(2)}, u32[]{:S(2)}) collective-permute-start(f32[32,128]{1,0:T(8,128)S(1)} %get-tuple-element.169), channel_id=1, source_target_pairs={{0,1},{1,0},{2,3},{3,2},{4,5},{5,4},{6,7},{7,6},{8,9},{9,8},{10,11... | collective-permute-start | bytes 49160 | tf_op jit(solution)/shard_map/ppermute | solution.py:673
  (30 other events, 230.8 us)
where the time goes:
time: 110 us
  starting transfers between devices  53.2 us (48%)
  waiting for transfers between devices  27.8 us (25%)
  Pallas kernels  27.5 us (25%)
  between operations  1.23 us (1%)
    ppermute x22, starting transfers between devices, swap_far(): lax.ppermute(face, axis, [(i, far_partner(i, size)) for i in range(size)])  32.8 us
    pallas_call x24, Pallas kernels, call(): pl.pallas_call(kernel, name=name, out_shape=[jax.ShapeDtypeStruct(s, jnp....  27.5 us
    ppermute x22, waiting for transfers between devices, swap_far(): lax.ppermute(face, axis, [(i, far_partner(i, size)) for i in range(size)])  15.9 us
    ppermute x22, starting transfers between devices, swap_near(): lax.ppermute(face, axis, [(i, i ^ 1) for i in range(lax.axis_size(axis))])  12.6 us
    ppermute x7, starting transfers between devices, partner_sum(): load = lax.ppermute(load, axis, [(i, partner(i)) for i in range(size)])  7.79 us
    ppermute x7, waiting for transfers between devices, partner_sum(): load = lax.ppermute(load, axis, [(i, partner(i)) for i in range(size)])  6.82 us
    ppermute x22, waiting for transfers between devices, swap_near(): lax.ppermute(face, axis, [(i, i ^ 1) for i in range(lax.axis_size(axis))])  5.05 us
  transfers between devices with their start and end apart: 51, of which 20 were waited for; matrix products, arithmetic and copies ran while one was open for 0% of the time, Pallas kernels for 14%

commit v1 on v0

--- a/solution.py
+++ b/solution.py
@@ -686,6 +686,20 @@
     return x_far, x_near, y_far, y_near
 
 
+def swap_together(x_near, x_far, y_near, y_far):
+    size, me = lax.axis_size("gx"), lax.axis_index("gx")
+    place = jnp.arange(size)
+    near = (place == me ^ 1)[:, None, None]
+    far = (place == jnp.where(me % 2 == 1, me + 1, me - 1) % size)[:, None, None]
+    load = jnp.where(near, x_near[None], jnp.where(far, x_far[None], 0.0))
+    y_far = swap_far("gy", y_far)
+    y_near = swap_near("gy", y_near)
+    load = lax.all_to_all(load, "gx", 0, 0)
+    x_near = jnp.sum(jnp.where(near, load, 0.0), axis=0)
+    x_far = jnp.sum(jnp.where(far, load, 0.0), axis=0)
+    return x_far, x_near, y_far, y_near
+
+
 def far_partner(i, size):
     return (i + 1 if i % 2 else i - 1) % size
 
@@ -838,7 +852,7 @@
     pressure = update
     for step in range(1, CHEB):
         last = step == CHEB - 1
-        received = swap_all(*sent)
+        received = swap_together(*sent)
         (raw,) = call(
             pressure_sums, "pressure_sums", [brick],
             update, t.summed, t.shift, t.stiff_y, t.stiff_z, cost=busy(2 << 20),

time: 110 us -> 162 us (1.47); the launches traced: 110 us -> 159 us
  local copies, waits for them, and re-layouts: 0.15 us -> 33.8 us
  other arithmetic: 0.04 us -> 7.36 us
  starting transfers between devices: 53.2 us -> 59.1 us
  waiting for transfers between devices: 27.8 us -> 29.6 us
    unnamed x22 -> x144, local copies, waits for them, and re-layouts: 0.07 us -> 31.6 us
    all_to_all x0 -> x5, starting transfers between devices: none -> 19.7 us  [swap_together(): load = lax.all_to_all(load, 'gx', 0, 0)]
    all_to_all x0 -> x5, waiting for transfers between devices: none -> 13.4 us  [swap_together(): load = lax.all_to_all(load, 'gx', 0, 0)]
    ppermute x22 -> x17, waiting for transfers between devices: 15.9 us -> 7.39 us  [swap_far(): lax.ppermute(face, axis, [(i, far_partner(i, size)) for i in range(size)])]
    ppermute x22 -> x17, starting transfers between devices: 32.8 us -> 25.6 us  [swap_far(): lax.ppermute(face, axis, [(i, far_partner(i, size)) for i in range(size)])]
    ppermute x22 -> x17, starting transfers between devices: 12.6 us -> 6.18 us  [swap_near(): lax.ppermute(face, axis, [(i, i ^ 1) for i in range(lax.axis_size(axis))])]
    select_n x0 -> x5, other arithmetic: none -> 3.46 us  [swap_together(): load = jnp.where(near, x_near[None], jnp.where(far, x_far[None], 0.0))]
    ppermute x22 -> x17, waiting for transfers between devices: 5.05 us -> 2.68 us  [swap_near(): lax.ppermute(face, axis, [(i, i ^ 1) for i in range(lax.axis_size(axis))])]
  transfers between devices with their start and end apart: 51 -> 46, of which waited for: 20 -> 18; matrix products, arithmetic and copies ran while one was open for 0% -> 2% of each run, Pallas kernels for 14% -> 10%
where the time goes in v1:
time: 162 us; the launch traced here: 159 us
  starting transfers between devices  59.1 us (36%)
  local copies, waits for them, and re-layouts  33.8 us (21%)
  waiting for transfers between devices  29.6 us (18%)
  Pallas kernels  27.9 us (17%)
  other arithmetic  7.36 us (5%)
    unnamed x144, local copies, waits for them, and re-layouts  31.6 us
    pallas_call x24, Pallas kernels, call(): pl.pallas_call(kernel, name=name, out_shape=[jax.ShapeDtypeStruct(s, jnp....  27.9 us
    ppermute x17, starting transfers between devices, swap_far(): lax.ppermute(face, axis, [(i, far_partner(i, size)) for i in range(size)])  25.6 us
    all_to_all x5, starting transfers between devices, swap_together(): load = lax.all_to_all(load, 'gx', 0, 0)  19.7 us
    all_to_all x5, waiting for transfers between devices, swap_together(): load = lax.all_to_all(load, 'gx', 0, 0)  13.4 us
    ppermute x7, starting transfers between devices, partner_sum(): load = lax.ppermute(load, axis, [(i, partner(i)) for i in range(size)])  7.66 us
    ppermute x17, waiting for transfers between devices, swap_far(): lax.ppermute(face, axis, [(i, far_partner(i, size)) for i in range(size)])  7.39 us
    ppermute x17, starting transfers between devices, swap_near(): lax.ppermute(face, axis, [(i, i ^ 1) for i in range(lax.axis_size(axis))])  6.18 us
  transfers between devices with their start and end apart: 46, of which 18 were waited for; matrix products, arithmetic and copies ran while one was open for 2% of the time, Pallas kernels for 10%

profile of v1, /device:TPU:0, one launch (start us, length us, event | category | flops | bytes accessed | tf_op | source)
XLA Modules:
  0.0 159.2 jit_solution(2542274365841064730)
XLA Ops:
  0.7 2.0 %local_right.1 = (f32[5,32,16,128]{3,2,1,0:T(8,128)S(1)}, f32[5,16,128]{2,1,0:T(8,128)S(1)}, f32[5,16,128]{2,1,0:T(8,128)S(1)}, f32[5,32,128]{2,1,0:T(8,128)S(1)}, f32[5,32,128]{2,1,0:T(8,128)S(1)}) custom-call(f32[4,32,16,128]{3,2,1,0:T(8,128)} %old_far.1, f32[32,16,128]{2,1,0:T(8,128)} %step_far.1, f32[2,8,128]{2,1,0:T(8,128)S(1)} %stack.9.even_ref.refs_8_.refs_31_.refs_6_), custom_call_target="tpu_custom_call" | custom-call | tf_op jit(solution)/shard_map/local_right/pallas_call | solution.py:656
  2.8 4.0 %collective-permute-start = (f32[5,16,128]{2,1,0:T(8,128)S(1)}, f32[5,16,128]{2,1,0:T(8,128)S(1)}, u32[]{:S(2)}, u32[]{:S(2)}) collective-permute-start(f32[5,16,128]{2,1,0:T(8,128)S(1)} %get-tuple-element.88), channel_id=1, source_target_pairs={{0,24},{8,16},{16,8},{24,0},{1,25},{9,17},{17,9},{25,1},{2,26},{10... | collective-permute-start | bytes 122888 | tf_op jit(solution)/shard_map/ppermute | solution.py:678
  8.7 2.0 %collective-permute-done.1.x_near = f32[5,16,128]{2,1,0:T(8,128)S(1)} collective-permute-done((f32[5,16,128]{2,1,0:T(8,128)S(1)}, f32[5,16,128]{2,1,0:T(8,128)S(1)}, u32[]{:S(2)}, u32[]{:S(2)}) %collective-permute-start.1) | collective-permute-done | bytes 40992 | tf_op jit(solution)/shard_map/ppermute | solution.py:673
  10.8 2.2 %collective-permute-start.2 = (f32[5,32,128]{2,1,0:T(8,128)S(1)}, f32[5,32,128]{2,1,0:T(8,128)S(1)}, u32[]{:S(2)}, u32[]{:S(2)}) collective-permute-start(f32[5,32,128]{2,1,0:T(8,128)S(1)} %get-tuple-element.92), channel_id=1, source_target_pairs={{0,7},{1,2},{2,1},{3,4},{4,3},{5,6},{6,5},{7,0},{8,15},{9,10},{10,... | collective-permute-start | bytes 245768 | tf_op jit(solution)/shard_map/ppermute | solution.py:678
  13.0 4.1 %collective-permute-done.2.y_far = f32[5,32,128]{2,1,0:T(8,128)S(1)} collective-permute-done((f32[5,32,128]{2,1,0:T(8,128)S(1)}, f32[5,32,128]{2,1,0:T(8,128)S(1)}, u32[]{:S(2)}, u32[]{:S(2)}) %collective-permute-start.2) | collective-permute-done | bytes 81952 | tf_op jit(solution)/shard_map/ppermute | solution.py:678
  21.3 2.6 %right_sums.1 = (f32[32,16,128]{2,1,0:T(8,128)S(1)}, f32[32,16,128]{2,1,0:T(8,128)S(1)}, f32[4,32,16,128]{3,2,1,0:T(8,128)S(1)}, f32[8,128]{1,0:T(8,128)S(1)}) custom-call(f32[5,32,16,128]{3,2,1,0:T(8,128)S(1)} %get-tuple-element.87.local, s32[32,16,128]{2,1,0:T(8,128)S(1)} %copy-done.16, f32[5,16,128]{2,1,0:T(8,128)S(1)} %collective-permute-done.x_far, ...), custom_call_target="tpu_custom_call" | custom-call | bytes 8388608 | tf_op jit(solution)/shard_map/right_sums/pallas_call | solution.py:656
  26.2 2.0 %collective-permute-start.8 = (f32[5,16,128]{2,1,0:T(8,128)S(1)}, f32[5,16,128]{2,1,0:T(8,128)S(1)}, u32[]{:S(2)}, u32[]{:S(2)}) collective-permute-start(f32[5,16,128]{2,1,0:T(8,128)S(1)} %get-tuple-element.104), channel_id=1, source_target_pairs={{0,24},{8,16},{16,8},{24,0},{1,25},{9,17},{17,9},{25,1},{2,26},{10... | collective-permute-start | bytes 122888 | tf_op jit(solution)/shard_map/ppermute | solution.py:678
  29.3 2.6 %basis_sums.4 = (f32[4,32,16,128]{3,2,1,0:T(8,128)S(1)}, f32[8,128]{1,0:T(8,128)S(1)}) custom-call(f32[4,32,16,128]{3,2,1,0:T(8,128)S(1)} %get-tuple-element.101.newest.older.refs_2_, f32[4,32,16,128]{3,2,1,0:T(8,128)S(1)} %get-tuple-element.94.right.older.refs_1_, f32[32,16,128]{2,1,0:T(8,128)S(1)} %get-tuple-element.102.reaction.refs_2_, ...), custom_call_target="tpu_custom_call" | custom-call | bytes 8388608 | tf_op jit(solution)/shard_map/basis_sums/pallas_call | solution.py:656
  32.9 1.8 %collective-permute-start.14 = (f32[5,32,128]{2,1,0:T(8,128)S(1)}, f32[5,32,128]{2,1,0:T(8,128)S(1)}, u32[]{:S(2)}, u32[]{:S(2)}) collective-permute-start(f32[5,32,128]{2,1,0:T(8,128)S(1)} %get-tuple-element.112), channel_id=1, source_target_pairs={{0,7},{1,2},{2,1},{3,4},{4,3},{5,6},{6,5},{7,0},{8,15},{9,10},{10,... | collective-permute-start | bytes 245768 | tf_op jit(solution)/shard_map/ppermute | solution.py:678
  36.9 2.6 %basis_sums.5 = (f32[4,32,16,128]{3,2,1,0:T(8,128)S(1)}, f32[8,128]{1,0:T(8,128)S(1)}) custom-call(f32[4,32,16,128]{3,2,1,0:T(8,128)S(1)} %get-tuple-element.108.newest.older.refs_3_, f32[4,32,16,128]{3,2,1,0:T(8,128)S(1)} %get-tuple-element.101.newest.older.refs_2_, f32[32,16,128]{2,1,0:T(8,128)S(1)} %get-tuple-element.102.reaction.refs_2_, ...), custom_call_target="tpu_custom_call" | custom-call | bytes 8388608 | tf_op jit(solution)/shard_map/basis_sums/pallas_call | solution.py:656
  41.8 1.7 %collective-permute-start.16 = (f32[5,16,128]{2,1,0:T(8,128)S(1)}, f32[5,16,128]{2,1,0:T(8,128)S(1)}, u32[]{:S(2)}, u32[]{:S(2)}) collective-permute-start(f32[5,16,128]{2,1,0:T(8,128)S(1)} %get-tuple-element.116), channel_id=1, source_target_pairs={{0,24},{8,16},{16,8},{24,0},{1,25},{9,17},{17,9},{25,1},{2,26},{10... | collective-permute-start | bytes 122888 | tf_op jit(solution)/shard_map/ppermute | solution.py:678
  44.5 2.6 %basis_sums.6 = (f32[4,32,16,128]{3,2,1,0:T(8,128)S(1)}, f32[8,128]{1,0:T(8,128)S(1)}) custom-call(f32[4,32,16,128]{3,2,1,0:T(8,128)S(1)} %get-tuple-element.114.newest.older.refs_4_, f32[4,32,16,128]{3,2,1,0:T(8,128)S(1)} %get-tuple-element.108.newest.older.refs_3_, f32[32,16,128]{2,1,0:T(8,128)S(1)} %get-tuple-element.102.reaction.refs_2_, ...), custom_call_target="tpu_custom_call" | custom-call | bytes 8388608 | tf_op jit(solution)/shard_map/basis_sums/pallas_call | solution.py:656
  48.2 1.8 %collective-permute-start.22 = (f32[5,32,128]{2,1,0:T(8,128)S(1)}, f32[5,32,128]{2,1,0:T(8,128)S(1)}, u32[]{:S(2)}, u32[]{:S(2)}) collective-permute-start(f32[5,32,128]{2,1,0:T(8,128)S(1)} %get-tuple-element.124), channel_id=1, source_target_pairs={{0,7},{1,2},{2,1},{3,4},{4,3},{5,6},{6,5},{7,0},{8,15},{9,10},{10,... | collective-permute-start | bytes 245768 | tf_op jit(solution)/shard_map/ppermute | solution.py:678
  52.2 2.6 %basis_sums.7 = (f32[4,32,16,128]{3,2,1,0:T(8,128)S(1)}, f32[8,128]{1,0:T(8,128)S(1)}) custom-call(f32[4,32,16,128]{3,2,1,0:T(8,128)S(1)} %get-tuple-element.120.newest.refs_1_.refs_5_, f32[4,32,16,128]{3,2,1,0:T(8,128)S(1)} %get-tuple-element.114.newest.older.refs_4_, f32[32,16,128]{2,1,0:T(8,128)S(1)} %get-tuple-element.102.reaction.refs_2_, ...), custom_call_target="tpu_custom_call" | custom-call | bytes 8388608 | tf_op jit(solution)/shard_map/basis_sums/pallas_call | solution.py:656
  55.1 2.6 %last_field.1 = (f32[4,32,16,128]{3,2,1,0:T(8,128)S(1)}, f32[6,8,128]{2,1,0:T(8,128)S(1)}, f32[16,128]{1,0:T(8,128)S(1)}, f32[16,128]{1,0:T(8,128)S(1)}, f32[32,128]{1,0:T(8,128)S(1)}, /*index=5*/f32[32,128]{1,0:T(8,128)S(1)}) custom-call(f32[4,32,16,128]{3,2,1,0:T(8,128)S(1)} %get-tuple-element.121.refs_0_, ...), custom_call_target="tpu_custom_call" | custom-call | tf_op jit(solution)/shard_map/last_field/pallas_call | solution.py:656
  58.8 1.9 %collective-permute-start.24 = (f32[64,128]{1,0:T(8,128)S(1)}, f32[64,128]{1,0:T(8,128)S(1)}, u32[]{:S(2)}, u32[]{:S(2)}) collective-permute-start(f32[64,128]{1,0:T(8,128)S(1)} %get-tuple-element.182), channel_id=1, source_target_pairs={{0,24},{8,16},{16,8},{24,0},{1,25},{9,17},{17,9},{25,1},{2,26},{10... | collective-permute-start | bytes 98312 | tf_op jit(solution)/shard_map/ppermute | solution.py:712
  62.3 3.1 %collective-permute-done.26 = f32[48,128]{1,0:T(8,128)S(1)} collective-permute-done((f32[48,128]{1,0:T(8,128)S(1)}, f32[48,128]{1,0:T(8,128)S(1)}, u32[]{:S(2)}, u32[]{:S(2)}) %collective-permute-start.26) | collective-permute-done | bytes 24608 | tf_op jit(solution)/shard_map/ppermute | solution.py:712
  67.5 2.0 %collective-permute-start.29 = (f32[48,128]{1,0:T(8,128)}, f32[48,128]{1,0:T(8,128)}, u32[]{:S(2)}, u32[]{:S(2)}) collective-permute-start(f32[48,128]{1,0:T(8,128)} %fusion.2), channel_id=1, source_target_pairs={{0,3},{1,6},{2,5},{3,0},{4,7},{5,2},{6,1},{7,4},{8,11},{9,14},{10,... | collective-permute-start | bytes 73736 | tf_op jit(solution)/shard_map/ppermute | solution.py:712
  69.5 2.1 %collective-permute-start.28 = (f32[48,128]{1,0:T(8,128)}, f32[48,128]{1,0:T(8,128)}, u32[]{:S(2)}, u32[]{:S(2)}) collective-permute-start(f32[48,128]{1,0:T(8,128)} %fusion.2), channel_id=1, source_target_pairs={{0,4},{1,5},{2,6},{3,7},{4,0},{5,1},{6,2},{7,3},{8,12},{9,13},{10,... | collective-permute-start | bytes 73736 | tf_op jit(solution)/shard_map/ppermute | solution.py:712
  71.6 3.0 %collective-permute-done.28 = f32[48,128]{1,0:T(8,128)} collective-permute-done((f32[48,128]{1,0:T(8,128)}, f32[48,128]{1,0:T(8,128)}, u32[]{:S(2)}, u32[]{:S(2)}) %collective-permute-start.28) | collective-permute-done | bytes 24608 | tf_op jit(solution)/shard_map/ppermute | solution.py:712
  100.9 2.5 %fields.1 = (f32[4,32,16,128]{3,2,1,0:T(8,128)}, f32[32,16,128]{2,1,0:T(8,128)S(1)}, f32[32,16,128]{2,1,0:T(8,128)S(1)}, f32[16,128]{1,0:T(8,128)S(1)}, f32[16,1...) custom-call(f32[6,8,128]{2,1,0:T(8,128)S(1)} %fusion.refs_0_, ...), custom_call_target="tpu_custom_call" | custom-call | tf_op jit(solution)/shard_map/fields/pallas_call | solution.py:656
  106.7 3.3 %all-to-all-start = ((f32[4,16,128]{2,1,0:T(8,128)}), f32[4,16,128]{2,1,0:T(8,128)S(1)}, u32[]{:S(2)}, u32[]{:S(2)}) async-start(f32[4,16,128]{2,1,0:T(8,128)} %select_select_fusion.4), calls=%async_computation | async-start | bytes 65536 | tf_op jit(solution)/shard_map/all_to_all | solution.py:697
  110.0 2.5 %collective-permute-start.31 = (f32[32,128]{1,0:T(8,128)}, f32[32,128]{1,0:T(8,128)S(1)}, u32[]{:S(2)}, u32[]{:S(2)}) collective-permute-start(f32[32,128]{1,0:T(8,128)} %copy-done.69), channel_id=1, source_target_pairs={{0,7},{1,2},{2,1},{3,4},{4,3},{5,6},{6,5},{7,0},{8,15},{9,10},{10,... | collective-permute-start | bytes 49160 | tf_op jit(solution)/shard_map/ppermute | solution.py:678
  119.3 3.8 %all-to-all-start.1 = ((f32[4,16,128]{2,1,0:T(8,128)}), f32[4,16,128]{2,1,0:T(8,128)S(1)}, u32[]{:S(2)}, u32[]{:S(2)}) async-start(f32[4,16,128]{2,1,0:T(8,128)} %select_select_fusion.3), calls=%async_computation.1 | async-start | bytes 65536 | tf_op jit(solution)/shard_map/all_to_all | solution.py:697
  123.1 1.7 %collective-permute-start.33 = (f32[32,128]{1,0:T(8,128)S(1)}, f32[32,128]{1,0:T(8,128)S(1)}, u32[]{:S(2)}, u32[]{:S(2)}) collective-permute-start(f32[32,128]{1,0:T(8,128)S(1)} %get-tuple-element.147), channel_id=1, source_target_pairs={{0,7},{1,2},{2,1},{3,4},{4,3},{5,6},{6,5},{7,0},{8,15},{9,10},{10,... | collective-permute-start | bytes 49160 | tf_op jit(solution)/shard_map/ppermute | solution.py:678
  125.4 2.5 %all-to-all-done.1 = f32[4,16,128]{2,1,0:T(8,128)S(1)} async-done(((f32[4,16,128]{2,1,0:T(8,128)}), f32[4,16,128]{2,1,0:T(8,128)S(1)}, u32[]{:S(2)}, u32[]{:S(2)}) %all-to-all-start.1) | async-done | bytes 32800 | tf_op jit(solution)/shard_map/all_to_all | solution.py:697
  129.0 4.2 %all-to-all-start.2 = ((f32[4,16,128]{2,1,0:T(8,128)}), f32[4,16,128]{2,1,0:T(8,128)S(1)}, u32[]{:S(2)}, u32[]{:S(2)}) async-start(f32[4,16,128]{2,1,0:T(8,128)} %select_select_fusion.2), calls=%async_computation.2 | async-start | bytes 65536 | tf_op jit(solution)/shard_map/all_to_all | solution.py:697
  134.8 3.1 %all-to-all-done.2 = f32[4,16,128]{2,1,0:T(8,128)S(1)} async-done(((f32[4,16,128]{2,1,0:T(8,128)}), f32[4,16,128]{2,1,0:T(8,128)S(1)}, u32[]{:S(2)}, u32[]{:S(2)}) %all-to-all-start.2) | async-done | bytes 32800 | tf_op jit(solution)/shard_map/all_to_all | solution.py:697
  139.0 4.2 %all-to-all-start.3 = ((f32[4,16,128]{2,1,0:T(8,128)}), f32[4,16,128]{2,1,0:T(8,128)S(1)}, u32[]{:S(2)}, u32[]{:S(2)}) async-start(f32[4,16,128]{2,1,0:T(8,128)} %select_select_fusion.1), calls=%async_computation.3 | async-start | bytes 65536 | tf_op jit(solution)/shard_map/all_to_all | solution.py:697
  144.3 3.6 %all-to-all-done.3 = f32[4,16,128]{2,1,0:T(8,128)S(1)} async-done(((f32[4,16,128]{2,1,0:T(8,128)}), f32[4,16,128]{2,1,0:T(8,128)S(1)}, u32[]{:S(2)}, u32[]{:S(2)}) %all-to-all-start.3) | async-done | bytes 32800 | tf_op jit(solution)/shard_map/all_to_all | solution.py:697
  149.1 4.2 %all-to-all-start.4 = ((f32[4,16,128]{2,1,0:T(8,128)}), f32[4,16,128]{2,1,0:T(8,128)S(1)}, u32[]{:S(2)}, u32[]{:S(2)}) async-start(f32[4,16,128]{2,1,0:T(8,128)} %select_select_fusion), calls=%async_computation.4 | async-start | bytes 65536 | tf_op jit(solution)/shard_map/all_to_all | solution.py:697
  153.9 4.2 %all-to-all-done.4 = f32[4,16,128]{2,1,0:T(8,128)S(1)} async-done(((f32[4,16,128]{2,1,0:T(8,128)}), f32[4,16,128]{2,1,0:T(8,128)S(1)}, u32[]{:S(2)}, u32[]{:S(2)}) %all-to-all-start.4) | async-done | bytes 32800 | tf_op jit(solution)/shard_map/all_to_all | solution.py:697
  (251 shorter events, 68.6 us)
Async XLA Ops:
  2.8 5.9 %collective-permute-start = (f32[5,16,128]{2,1,0:T(8,128)S(1)}, f32[5,16,128]{2,1,0:T(8,128)S(1)}, u32[]{:S(2)}, u32[]{:S(2)}) collective-permute-start(f32[5,16,128]{2,1,0:T(8,128)S(1)} %get-tuple-element.88), channel_id=1, source_target_pairs={{0,24},{8,16},{16,8},{24,0},{1,25},{9,17},{17,9},{25,1},{2,26},{10... | collective-permute-start | bytes 122888 | tf_op jit(solution)/shard_map/ppermute | solution.py:678
  10.8 6.3 %collective-permute-start.2 = (f32[5,32,128]{2,1,0:T(8,128)S(1)}, f32[5,32,128]{2,1,0:T(8,128)S(1)}, u32[]{:S(2)}, u32[]{:S(2)}) collective-permute-start(f32[5,32,128]{2,1,0:T(8,128)S(1)} %get-tuple-element.92), channel_id=1, source_target_pairs={{0,7},{1,2},{2,1},{3,4},{4,3},{5,6},{6,5},{7,0},{8,15},{9,10},{10,... | collective-permute-start | bytes 245768 | tf_op jit(solution)/shard_map/ppermute | solution.py:678
  17.8 6.9 %collective-permute-start.6 = (f32[5,32,128]{2,1,0:T(8,128)S(1)}, f32[5,32,128]{2,1,0:T(8,128)S(1)}, u32[]{:S(2)}, u32[]{:S(2)}) collective-permute-start(f32[5,32,128]{2,1,0:T(8,128)S(1)} %get-tuple-element.99), channel_id=1, source_target_pairs={{0,7},{1,2},{2,1},{3,4},{4,3},{5,6},{6,5},{7,0},{8,15},{9,10},{10,... | collective-permute-start | bytes 245768 | tf_op jit(solution)/shard_map/ppermute | solution.py:678
  19.4 5.3 %collective-permute-start.7 = (f32[5,32,128]{2,1,0:T(8,128)S(1)}, f32[5,32,128]{2,1,0:T(8,128)S(1)}, u32[]{:S(2)}, u32[]{:S(2)}) collective-permute-start(f32[5,32,128]{2,1,0:T(8,128)S(1)} %get-tuple-element.100), channel_id=1, source_target_pairs={{0,1},{1,0},{2,3},{3,2},{4,5},{5,4},{6,7},{7,6},{8,9},{9,8},{10,11... | collective-permute-start | bytes 245768 | tf_op jit(solution)/shard_map/ppermute | solution.py:673
  19.4 5.3 %collective-permute-start.4 = (f32[5,16,128]{2,1,0:T(8,128)S(1)}, f32[5,16,128]{2,1,0:T(8,128)S(1)}, u32[]{:S(2)}, u32[]{:S(2)}) collective-permute-start(f32[5,16,128]{2,1,0:T(8,128)S(1)} %get-tuple-element.97), channel_id=1, source_target_pairs={{0,24},{8,16},{16,8},{24,0},{1,25},{9,17},{17,9},{25,1},{2,26},{10... | collective-permute-start | bytes 122888 | tf_op jit(solution)/shard_map/ppermute | solution.py:678
  25.3 6.9 %collective-permute-start.10 = (f32[5,32,128]{2,1,0:T(8,128)S(1)}, f32[5,32,128]{2,1,0:T(8,128)S(1)}, u32[]{:S(2)}, u32[]{:S(2)}) collective-permute-start(f32[5,32,128]{2,1,0:T(8,128)S(1)} %get-tuple-element.106), channel_id=1, source_target_pairs={{0,7},{1,2},{2,1},{3,4},{4,3},{5,6},{6,5},{7,0},{8,15},{9,10},{10,... | collective-permute-start | bytes 245768 | tf_op jit(solution)/shard_map/ppermute | solution.py:678
  26.2 6.0 %collective-permute-start.11 = (f32[5,32,128]{2,1,0:T(8,128)S(1)}, f32[5,32,128]{2,1,0:T(8,128)S(1)}, u32[]{:S(2)}, u32[]{:S(2)}) collective-permute-start(f32[5,32,128]{2,1,0:T(8,128)S(1)} %get-tuple-element.107), channel_id=1, source_target_pairs={{0,1},{1,0},{2,3},{3,2},{4,5},{5,4},{6,7},{7,6},{8,9},{9,8},{10,11... | collective-permute-start | bytes 245768 | tf_op jit(solution)/shard_map/ppermute | solution.py:673
  26.2 5.7 %collective-permute-start.8 = (f32[5,16,128]{2,1,0:T(8,128)S(1)}, f32[5,16,128]{2,1,0:T(8,128)S(1)}, u32[]{:S(2)}, u32[]{:S(2)}) collective-permute-start(f32[5,16,128]{2,1,0:T(8,128)S(1)} %get-tuple-element.104), channel_id=1, source_target_pairs={{0,24},{8,16},{16,8},{24,0},{1,25},{9,17},{17,9},{25,1},{2,26},{10... | collective-permute-start | bytes 122888 | tf_op jit(solution)/shard_map/ppermute | solution.py:678
  32.9 7.0 %collective-permute-start.14 = (f32[5,32,128]{2,1,0:T(8,128)S(1)}, f32[5,32,128]{2,1,0:T(8,128)S(1)}, u32[]{:S(2)}, u32[]{:S(2)}) collective-permute-start(f32[5,32,128]{2,1,0:T(8,128)S(1)} %get-tuple-element.112), channel_id=1, source_target_pairs={{0,7},{1,2},{2,1},{3,4},{4,3},{5,6},{6,5},{7,0},{8,15},{9,10},{10,... | collective-permute-start | bytes 245768 | tf_op jit(solution)/shard_map/ppermute | solution.py:678
  34.7 5.2 %collective-permute-start.15 = (f32[5,32,128]{2,1,0:T(8,128)S(1)}, f32[5,32,128]{2,1,0:T(8,128)S(1)}, u32[]{:S(2)}, u32[]{:S(2)}) collective-permute-start(f32[5,32,128]{2,1,0:T(8,128)S(1)} %get-tuple-element.113), channel_id=1, source_target_pairs={{0,1},{1,0},{2,3},{3,2},{4,5},{5,4},{6,7},{7,6},{8,9},{9,8},{10,11... | collective-permute-start | bytes 245768 | tf_op jit(solution)/shard_map/ppermute | solution.py:673
  34.7 5.2 %collective-permute-start.12 = (f32[5,16,128]{2,1,0:T(8,128)S(1)}, f32[5,16,128]{2,1,0:T(8,128)S(1)}, u32[]{:S(2)}, u32[]{:S(2)}) collective-permute-start(f32[5,16,128]{2,1,0:T(8,128)S(1)} %get-tuple-element.110), channel_id=1, source_target_pairs={{0,24},{8,16},{16,8},{24,0},{1,25},{9,17},{17,9},{25,1},{2,26},{10... | collective-permute-start | bytes 122888 | tf_op jit(solution)/shard_map/ppermute | solution.py:678
  40.7 6.8 %collective-permute-start.18 = (f32[5,32,128]{2,1,0:T(8,128)S(1)}, f32[5,32,128]{2,1,0:T(8,128)S(1)}, u32[]{:S(2)}, u32[]{:S(2)}) collective-permute-start(f32[5,32,128]{2,1,0:T(8,128)S(1)} %get-tuple-element.118), channel_id=1, source_target_pairs={{0,7},{1,2},{2,1},{3,4},{4,3},{5,6},{6,5},{7,0},{8,15},{9,10},{10,... | collective-permute-start | bytes 245768 | tf_op jit(solution)/shard_map/ppermute | solution.py:678
  41.8 5.7 %collective-permute-start.19 = (f32[5,32,128]{2,1,0:T(8,128)S(1)}, f32[5,32,128]{2,1,0:T(8,128)S(1)}, u32[]{:S(2)}, u32[]{:S(2)}) collective-permute-start(f32[5,32,128]{2,1,0:T(8,128)S(1)} %get-tuple-element.119), channel_id=1, source_target_pairs={{0,1},{1,0},{2,3},{3,2},{4,5},{5,4},{6,7},{7,6},{8,9},{9,8},{10,11... | collective-permute-start | bytes 245768 | tf_op jit(solution)/shard_map/ppermute | solution.py:673
  41.8 5.3 %collective-permute-start.16 = (f32[5,16,128]{2,1,0:T(8,128)S(1)}, f32[5,16,128]{2,1,0:T(8,128)S(1)}, u32[]{:S(2)}, u32[]{:S(2)}) collective-permute-start(f32[5,16,128]{2,1,0:T(8,128)S(1)} %get-tuple-element.116), channel_id=1, source_target_pairs={{0,24},{8,16},{16,8},{24,0},{1,25},{9,17},{17,9},{25,1},{2,26},{10... | collective-permute-start | bytes 122888 | tf_op jit(solution)/shard_map/ppermute | solution.py:678
  48.2 6.9 %collective-permute-start.22 = (f32[5,32,128]{2,1,0:T(8,128)S(1)}, f32[5,32,128]{2,1,0:T(8,128)S(1)}, u32[]{:S(2)}, u32[]{:S(2)}) collective-permute-start(f32[5,32,128]{2,1,0:T(8,128)S(1)} %get-tuple-element.124), channel_id=1, source_target_pairs={{0,7},{1,2},{2,1},{3,4},{4,3},{5,6},{6,5},{7,0},{8,15},{9,10},{10,... | collective-permute-start | bytes 245768 | tf_op jit(solution)/shard_map/ppermute | solution.py:678
  49.9 5.1 %collective-permute-start.23 = (f32[5,32,128]{2,1,0:T(8,128)S(1)}, f32[5,32,128]{2,1,0:T(8,128)S(1)}, u32[]{:S(2)}, u32[]{:S(2)}) collective-permute-start(f32[5,32,128]{2,1,0:T(8,128)S(1)} %get-tuple-element.125), channel_id=1, source_target_pairs={{0,1},{1,0},{2,3},{3,2},{4,5},{5,4},{6,7},{7,6},{8,9},{9,8},{10,11... | collective-permute-start | bytes 245768 | tf_op jit(solution)/shard_map/ppermute | solution.py:673
  49.9 5.1 %collective-permute-start.20 = (f32[5,16,128]{2,1,0:T(8,128)S(1)}, f32[5,16,128]{2,1,0:T(8,128)S(1)}, u32[]{:S(2)}, u32[]{:S(2)}) collective-permute-start(f32[5,16,128]{2,1,0:T(8,128)S(1)} %get-tuple-element.122), channel_id=1, source_target_pairs={{0,24},{8,16},{16,8},{24,0},{1,25},{9,17},{17,9},{25,1},{2,26},{10... | collective-permute-start | bytes 122888 | tf_op jit(solution)/shard_map/ppermute | solution.py:678
  58.8 6.7 %collective-permute-start.24 = (f32[64,128]{1,0:T(8,128)S(1)}, f32[64,128]{1,0:T(8,128)S(1)}, u32[]{:S(2)}, u32[]{:S(2)}) collective-permute-start(f32[64,128]{1,0:T(8,128)S(1)} %get-tuple-element.182), channel_id=1, source_target_pairs={{0,24},{8,16},{16,8},{24,0},{1,25},{9,17},{17,9},{25,1},{2,26},{10... | collective-permute-start | bytes 98312 | tf_op jit(solution)/shard_map/ppermute | solution.py:712
  60.6 4.8 %collective-permute-start.25 = (f32[64,128]{1,0:T(8,128)S(1)}, f32[64,128]{1,0:T(8,128)S(1)}, u32[]{:S(2)}, u32[]{:S(2)}) collective-permute-start(f32[64,128]{1,0:T(8,128)S(1)} %get-tuple-element.183), channel_id=1, source_target_pairs={{0,8},{8,0},{16,24},{24,16},{1,9},{9,1},{17,25},{25,17},{2,10},{10... | collective-permute-start | bytes 98312 | tf_op jit(solution)/shard_map/ppermute | solution.py:712
  67.4 7.1 %collective-permute-start.27 = (f32[80,128]{1,0:T(8,128)}, f32[80,128]{1,0:T(8,128)}, u32[]{:S(2)}, u32[]{:S(2)}) collective-permute-start(f32[80,128]{1,0:T(8,128)} %pad_maximum_fusion), channel_id=1, source_target_pairs={{0,7},{1,2},{2,1},{3,4},{4,3},{5,6},{6,5},{7,0},{8,15},{9,10},{10,... | collective-permute-start | bytes 122888 | tf_op jit(solution)/shard_map/ppermute | solution.py:712
  69.5 5.1 %collective-permute-start.28 = (f32[48,128]{1,0:T(8,128)}, f32[48,128]{1,0:T(8,128)}, u32[]{:S(2)}, u32[]{:S(2)}) collective-permute-start(f32[48,128]{1,0:T(8,128)} %fusion.2), channel_id=1, source_target_pairs={{0,4},{1,5},{2,6},{3,7},{4,0},{5,1},{6,2},{7,3},{8,12},{9,13},{10,... | collective-permute-start | bytes 73736 | tf_op jit(solution)/shard_map/ppermute | solution.py:712
  106.7 8.9 %all-to-all-start = ((f32[4,16,128]{2,1,0:T(8,128)}), f32[4,16,128]{2,1,0:T(8,128)S(1)}, u32[]{:S(2)}, u32[]{:S(2)}) async-start(f32[4,16,128]{2,1,0:T(8,128)} %select_select_fusion.4), calls=%async_computation | async-start | bytes 65536 | tf_op jit(solution)/shard_map/all_to_all | solution.py:697
  110.0 5.7 %collective-permute-start.31 = (f32[32,128]{1,0:T(8,128)}, f32[32,128]{1,0:T(8,128)S(1)}, u32[]{:S(2)}, u32[]{:S(2)}) collective-permute-start(f32[32,128]{1,0:T(8,128)} %copy-done.69), channel_id=1, source_target_pairs={{0,7},{1,2},{2,1},{3,4},{4,3},{5,6},{6,5},{7,0},{8,15},{9,10},{10,... | collective-permute-start | bytes 49160 | tf_op jit(solution)/shard_map/ppermute | solution.py:678
  119.3 8.6 %all-to-all-start.1 = ((f32[4,16,128]{2,1,0:T(8,128)}), f32[4,16,128]{2,1,0:T(8,128)S(1)}, u32[]{:S(2)}, u32[]{:S(2)}) async-start(f32[4,16,128]{2,1,0:T(8,128)} %select_select_fusion.3), calls=%async_computation.1 | async-start | bytes 65536 | tf_op jit(solution)/shard_map/all_to_all | solution.py:697
  123.1 5.0 %collective-permute-start.33 = (f32[32,128]{1,0:T(8,128)S(1)}, f32[32,128]{1,0:T(8,128)S(1)}, u32[]{:S(2)}, u32[]{:S(2)}) collective-permute-start(f32[32,128]{1,0:T(8,128)S(1)} %get-tuple-element.147), channel_id=1, source_target_pairs={{0,7},{1,2},{2,1},{3,4},{4,3},{5,6},{6,5},{7,0},{8,15},{9,10},{10,... | collective-permute-start | bytes 49160 | tf_op jit(solution)/shard_map/ppermute | solution.py:678
  129.0 8.9 %all-to-all-start.2 = ((f32[4,16,128]{2,1,0:T(8,128)}), f32[4,16,128]{2,1,0:T(8,128)S(1)}, u32[]{:S(2)}, u32[]{:S(2)}) async-start(f32[4,16,128]{2,1,0:T(8,128)} %select_select_fusion.2), calls=%async_computation.2 | async-start | bytes 65536 | tf_op jit(solution)/shard_map/all_to_all | solution.py:697
  133.2 5.0 %collective-permute-start.35 = (f32[32,128]{1,0:T(8,128)S(1)}, f32[32,128]{1,0:T(8,128)S(1)}, u32[]{:S(2)}, u32[]{:S(2)}) collective-permute-start(f32[32,128]{1,0:T(8,128)S(1)} %get-tuple-element.154), channel_id=1, source_target_pairs={{0,7},{1,2},{2,1},{3,4},{4,3},{5,6},{6,5},{7,0},{8,15},{9,10},{10,... | collective-permute-start | bytes 49160 | tf_op jit(solution)/shard_map/ppermute | solution.py:678
  139.0 8.9 %all-to-all-start.3 = ((f32[4,16,128]{2,1,0:T(8,128)}), f32[4,16,128]{2,1,0:T(8,128)S(1)}, u32[]{:S(2)}, u32[]{:S(2)}) async-start(f32[4,16,128]{2,1,0:T(8,128)} %select_select_fusion.1), calls=%async_computation.3 | async-start | bytes 65536 | tf_op jit(solution)/shard_map/all_to_all | solution.py:697
  143.2 5.0 %collective-permute-start.37 = (f32[32,128]{1,0:T(8,128)S(1)}, f32[32,128]{1,0:T(8,128)S(1)}, u32[]{:S(2)}, u32[]{:S(2)}) collective-permute-start(f32[32,128]{1,0:T(8,128)S(1)} %get-tuple-element.161), channel_id=1, source_target_pairs={{0,7},{1,2},{2,1},{3,4},{4,3},{5,6},{6,5},{7,0},{8,15},{9,10},{10,... | collective-permute-start | bytes 49160 | tf_op jit(solution)/shard_map/ppermute | solution.py:678
  149.1 8.9 %all-to-all-start.4 = ((f32[4,16,128]{2,1,0:T(8,128)}), f32[4,16,128]{2,1,0:T(8,128)S(1)}, u32[]{:S(2)}, u32[]{:S(2)}) async-start(f32[4,16,128]{2,1,0:T(8,128)} %select_select_fusion), calls=%async_computation.4 | async-start | bytes 65536 | tf_op jit(solution)/shard_map/all_to_all | solution.py:697
  153.3 5.0 %collective-permute-start.39 = (f32[32,128]{1,0:T(8,128)S(1)}, f32[32,128]{1,0:T(8,128)S(1)}, u32[]{:S(2)}, u32[]{:S(2)}) collective-permute-start(f32[32,128]{1,0:T(8,128)S(1)} %get-tuple-element.168), channel_id=1, source_target_pairs={{0,7},{1,2},{2,1},{3,4},{4,3},{5,6},{6,5},{7,0},{8,15},{9,10},{10,... | collective-permute-start | bytes 49160 | tf_op jit(solution)/shard_map/ppermute | solution.py:678
  153.3 5.0 %collective-permute-start.40 = (f32[32,128]{1,0:T(8,128)S(1)}, f32[32,128]{1,0:T(8,128)S(1)}, u32[]{:S(2)}, u32[]{:S(2)}) collective-permute-start(f32[32,128]{1,0:T(8,128)S(1)} %get-tuple-element.169), channel_id=1, source_target_pairs={{0,1},{1,0},{2,3},{3,2},{4,5},{5,4},{6,7},{7,6},{8,9},{9,8},{10,11... | collective-permute-start | bytes 49160 | tf_op jit(solution)/shard_map/ppermute | solution.py:673
  (86 other events, 369.4 us)
